TPU v7x, 32 devices: a whole 2x2x4 slice. The times are simulated.
32 devices in a mesh: ray: 4 (over y, x), cell: 8 (over z, core).
Axes of the slice: x: 2, y: 2, z: 4, core: 2. Of those that a mesh axis runs over, the one named last changes fastest.
Arguments:
- probes: bfloat16 [4096, 128], P('cell'), may hold values from -6 to 6
- prior: float32 [4096], P('cell'), may hold values from 0.5 to 2
- tiles: bfloat16 [4, 8, 720, 128, 128], P('ray', 'cell'), may hold values from -0.078125 to 0.078125
- tile_ray: int32 [4, 8, 720], P('ray', 'cell'), may hold values from 0 to 15
- tile_cell: int32 [4, 8, 720], P('ray', 'cell'), may hold values from 0 to 31, as said below
- tile_count: int32 [4, 8], P('ray', 'cell'), may hold values from 360 to 720, as said below
- noise: float32 [4, 8, 2048], P('ray', 'cell'), may hold values from 0.25 to 4
Outputs:
- basis: float32 [4096, 128], P('cell')
- factor: float32 [128, 128], replicated
Inputs may be any that keep to these rules, and one draw needn't show every extreme that they name: `tile_count`: every device has between half of 720 and 720 live tile slots; in every draw some device has all 720 live. `tile_cell`: the slots of device (r, c) name only cell blocks of the owners c - 3 to c + 3 that exist, that is blocks max(c - 3, 0) * 4 up to (c + 4) * 4 - 1 or the last block.
All inputs are finite; a program needn't handle non-finite values.
Results may differ from a plain program's by a relative error of at most 0.0031.
Values may be sent and summed in bfloat16 or wider, within the bound.
A program may use at most 256 MiB of HBM per device.

v0:
```python
import jax
import jax.numpy as jnp
from jax import lax
from jax.sharding import PartitionSpec as P

REACH = 3


def passed_along(value, axis, by):
    length = lax.axis_size(axis)
    pairs = [(i, i + by) for i in range(length) if 0 <= i + by < length]
    return lax.ppermute(value, axis, pairs)


def local(probes, prior, tiles, tile_ray, tile_cell, tile_count, noise):
    tile_edge = tiles.shape[-1]
    probe_width = probes.shape[1]
    own_rows = probes.shape[0]
    own_blocks = own_rows // tile_edge
    owner_total = lax.axis_size("cell")
    owner_index = lax.axis_index("cell")
    span_blocks = (2 * REACH + 1) * own_blocks
    signed_offsets = [distance for distance in range(-REACH, REACH + 1) if distance != 0]
    scaled = (prior[:, None] * probes.astype(jnp.float32)).astype(jnp.bfloat16)
    fetched = {}
    for distance in signed_offsets:
        fetched[distance] = passed_along(scaled, "cell", -distance)
    fetched[0] = scaled
    window = jnp.concatenate([fetched[distance] for distance in range(-REACH, REACH + 1)], axis=0)
    window = window.reshape(span_blocks, tile_edge, probe_width)
    window_start = (owner_index - REACH) * own_blocks
    tile_set = tiles[0, 0]
    slot_total = tile_set.shape[0]
    ray_index = tile_ray[0, 0]
    local_block = tile_cell[0, 0] - window_start
    live_slot = jnp.arange(slot_total, dtype=jnp.int32) < tile_count[0, 0]
    ray_blocks = noise.shape[-1] // tile_edge
    padded = jnp.concatenate([window, jnp.zeros((1, tile_edge, probe_width), jnp.bfloat16)], axis=0)
    picked = padded[jnp.where(live_slot, local_block, span_blocks)]
    product = jnp.einsum("tij,tjk->tik", tile_set, picked, preferred_element_type=jnp.float32)
    forward = jax.ops.segment_sum(product, ray_index, num_segments=ray_blocks)
    weighted = (noise[0, 0].reshape(ray_blocks, tile_edge, 1) * forward).astype(jnp.bfloat16)
    wpadded = jnp.concatenate(
        [weighted, jnp.zeros((1, tile_edge, probe_width), jnp.bfloat16)], axis=0
    )
    back_rows = wpadded[jnp.where(live_slot, ray_index, ray_blocks)]
    backward = jnp.einsum("tij,tik->tjk", tile_set, back_rows, preferred_element_type=jnp.float32)
    window_rows = jax.ops.segment_sum(backward, local_block, num_segments=span_blocks)
    grouped = window_rows.reshape(2 * REACH + 1, own_rows, probe_width)
    owned_rows = grouped[REACH]
    for distance in signed_offsets:
        owned_rows = owned_rows + passed_along(grouped[REACH + distance], "cell", distance)
    root_cells = jnp.sqrt(jnp.float32(own_rows * owner_total))
    gradient = lax.psum(owned_rows, "ray")
    sample = prior[:, None] * gradient
    local_gram = jnp.dot(sample.T, sample, precision=lax.Precision.HIGHEST)
    gram_total = lax.psum(local_gram, "cell")
    lower_factor = jnp.linalg.cholesky(gram_total)
    basis_own = jax.scipy.linalg.solve_triangular(lower_factor, sample.T, lower=True).T
    return (basis_own * root_cells, lower_factor.T / root_cells)


def solution(mesh):
    placed = (
        P("cell", None),
        P("cell"),
        P("ray", "cell", None, None, None),
        P("ray", "cell", None),
        P("ray", "cell", None),
        P("ray", "cell"),
        P("ray", "cell", None),
    )
    return jax.shard_map(
        local, mesh=mesh, in_specs=placed, out_specs=(P("cell", None), P()), check_vma=False
    )
```

profile of v0, /device:TPU:0, one launch (start us, length us, event | category | flops | bytes accessed | tf_op | source)
XLA Modules:
  0.0 526.6 jit_solution(11728673975991126314)
XLA Ops:
  8.3 4.4 collective-permute-start
  12.6 3.5 collective-permute-start.1
  16.1 3.3 collective-permute-start.2
  19.5 1.3 collective-permute-start.3
  29.2 4.0 collective-permute-done.5
  33.3 18.1 %gather_fusion = bf16[720,128,128]{2,1,0:T(8,128)(2,1)} fusion(bf16[29,128,128]{2,1,0:T(8,128)(2,1)S(1)} %concatenate.10, s32[1024]{0:T(1024)S(1)} %get-tuple-element.16), kind=kCustom, calls=%fused_computation | custom fusion | bytes 47188800 | tf_op jit(solution)/shard_map/gather | solution.py:39
  51.4 30.6 %fusion.4 = f32[720,128,128]{2,1,0:T(8,128)} fusion(bf16[720,128,128]{2,1,0:T(8,128)(2,1)} %gather_fusion, bf16[1,1,720,128,128]{4,3,2,1,0:T(8,128)(2,1)} %param.9), kind=kOutput, calls=%fused_computation.8 | convolution fusion | flops 3019898880 | bytes 94371840 | tf_op jit(solution)/shard_map/tij,tjk->tik/dot_general | solution.py:40
  82.1 93.6 %scatter_fusion = f32[16,128,128]{2,1,0:T(8,128)S(1)} fusion(f32[16,128,128]{2,1,0:T(8,128)S(1)} %broadcast_in_dim.21, s32[720]{0:T(1024)S(1)} %reduce.7, f32[720,128,128]{2,1,0:T(8,128)} %fusion.4), kind=kCustom, calls=%fused_computation.2 | custom fusion | flops 11796480 | bytes 141560640 | tf_op jit(solution)/shard_map/scatter-add | solution.py:41
  176.2 18.0 %gather_fusion.1 = bf16[720,128,128]{2,1,0:T(8,128)(2,1)} fusion(bf16[17,128,128]{2,1,0:T(8,128)(2,1)S(1)} %concatenate.11, s32[1024]{0:T(1024)S(1)} %get-tuple-element.15), kind=kCustom, calls=%fused_computation.1 | custom fusion | bytes 47188800 | tf_op jit(solution)/shard_map/gather | solution.py:46
  194.2 29.4 %fusion.7 = f32[720,128,128]{1,2,0:T(8,128)} fusion(bf16[720,128,128]{2,1,0:T(8,128)(2,1)} %gather_fusion.1, bf16[1,1,720,128,128]{4,3,2,1,0:T(8,128)(2,1)} %param.9), kind=kOutput, calls=%fused_computation.9 | convolution fusion | flops 3019898880 | bytes 94371840 | tf_op jit(solution)/shard_map/tij,tik->tjk/dot_general | solution.py:47
  223.6 45.8 %copy.15 = f32[720,128,128]{2,1,0:T(8,128)} copy(f32[720,128,128]{1,2,0:T(8,128)} %fusion.7) | data formatting | bytes 94371840 | tf_op jit(solution)/shard_map/tij,tik->tjk/dot_general | solution.py:47
  269.6 93.6 %scatter_fusion.1 = f32[28,128,128]{2,1,0:T(8,128)S(1)} fusion(f32[28,128,128]{2,1,0:T(8,128)S(1)} %broadcast_in_dim.20, s32[720]{0:T(1024)S(1)} %subtract_reduce_fusion, f32[720,128,128]{2,1,0:T(8,128)} %copy.15), kind=kCustom, calls=%fused_computation.3 | custom fusion | flops 11796480 | bytes 141560640 | tf_op jit(solution)/shard_map/scatter-add | solution.py:48
  363.3 5.3 %collective-permute-start.10 = (f32[512,128]{1,0:T(8,128)S(1)}, f32[512,128]{1,0:T(8,128)S(1)}, u32[]{:S(2)}, u32[]{:S(2)}) collective-permute-start(f32[512,128]{1,0:T(8,128)S(1)} %bitcast.59), channel_id=1, source_target_pairs={{0,2},{1,3},{2,4},{3,5},{4,6},{5,7},{8,10},{9,11},{10,12},{11,13},... | collective-permute-start | bytes 786440 | tf_op jit(solution)/shard_map/ppermute | solution.py:12
  368.7 3.9 collective-permute-start.11
  372.6 1.5 collective-permute-start.6
  376.7 3.3 collective-permute-start.9
  380.0 1.5 collective-permute-done.6
  381.5 6.5 %collective-permute-done.7 = f32[512,128]{1,0:T(8,128)S(1)} collective-permute-done((f32[512,128]{1,0:T(8,128)S(1)}, f32[512,128]{1,0:T(8,128)S(1)}, u32[]{:S(2)}, u32[]{:S(2)}) %collective-permute-start.7) | collective-permute-done | bytes 262176 | tf_op jit(solution)/shard_map/ppermute | solution.py:12
  388.9 46.9 %all-reduce.5.cloned.1.call-done = f32[512,128]{1,0:T(8,128)} async-done(((f32[512,128]{1,0:T(8,128)}), f32[512,128]{1,0:T(8,128)}) %all-reduce.5.cloned.1.call-update) | async-done | bytes 262160 | tf_op jit(solution)/shard_map/psum | solution.py:54
  435.7 2.4 fusion.16
  438.2 54.2 %all-reduce.7.cloned.1.call-done = f32[128,128]{0,1:T(8,128)} async-done(((f32[128,128]{0,1:T(8,128)}), f32[128,128]{0,1:T(8,128)}) %all-reduce.7.cloned.1.call-update) | async-done | bytes 65552 | tf_op jit(solution)/shard_map/psum | solution.py:57
  494.1 11.7 %cholesky.16 = f32[128,128]{1,0:T(8,128)S(1)} custom-call(f32[128,128]{1,0:T(8,128)S(1)} %fusion.21), custom_call_target="Cholesky" | custom-call | tf_op jit(solution)/shard_map/jit(cholesky)/cholesky | solution.py:58
  507.2 9.8 %custom-call.7 = f32[1,128,128]{1,2,0:T(8,128)S(1)} custom-call(f32[1,128,128]{2,1,0:T(8,128)S(1)} %get-tuple-element.14), custom_call_target="InvertDiagBlocksLowerTriangular" | custom-call | tf_op jit(solution)/shard_map/jit(_solve_triangular)/triangular_solve | solution.py:59
  517.7 2.1 convolution_multiply_fusion
  (47 shorter events, 17.0 us)
Async XLA Ops:
  7.2 428.6 %all-reduce.5.cloned.1.call-start = ((), (), s32[]{:S(2)}) async-start(), calls=%async_computation | async-start | bytes 524288 | tf_op jit(solution)/shard_map/psum | solution.py:54
  8.3 17.3 %collective-permute-start = (bf16[512,128]{1,0:T(8,128)(2,1)S(1)}, bf16[512,128]{1,0:T(8,128)(2,1)S(1)}, u32[]{:S(2)}, u32[]{:S(2)}) collective-permute-start(bf16[512,128]{1,0:T(8,128)(2,1)S(1)} %multiply_convert_fusion.1), channel_id=1, source_target_pairs={{0,3},{1,4},{2,5},{3,6},{4,7},{8,11},{9,12},{10,13},{11,14},{12,15... | collective-permute-start | bytes 393224 | tf_op jit(solution)/shard_map/ppermute | solution.py:12
  12.6 14.2 %collective-permute-start.1 = (bf16[512,128]{1,0:T(8,128)(2,1)S(1)}, bf16[512,128]{1,0:T(8,128)(2,1)S(1)}, u32[]{:S(2)}, u32[]{:S(2)}) collective-permute-start(bf16[512,128]{1,0:T(8,128)(2,1)S(1)} %multiply_convert_fusion.1), channel_id=1, source_target_pairs={{0,2},{1,3},{2,4},{3,5},{4,6},{5,7},{8,10},{9,11},{10,12},{11,13},... | collective-permute-start | bytes 393224 | tf_op jit(solution)/shard_map/ppermute | solution.py:12
  16.1 10.8 %collective-permute-start.2 = (bf16[512,128]{1,0:T(8,128)(2,1)S(1)}, bf16[512,128]{1,0:T(8,128)(2,1)S(1)}, u32[]{:S(2)}, u32[]{:S(2)}) collective-permute-start(bf16[512,128]{1,0:T(8,128)(2,1)S(1)} %multiply_convert_fusion.1), channel_id=1, source_target_pairs={{0,1},{1,2},{2,3},{3,4},{4,5},{5,6},{6,7},{8,9},{9,10},{10,11},{11... | collective-permute-start | bytes 393224 | tf_op jit(solution)/shard_map/ppermute | solution.py:12
  19.5 8.6 %collective-permute-start.3 = (bf16[512,128]{1,0:T(8,128)(2,1)S(1)}, bf16[512,128]{1,0:T(8,128)(2,1)S(1)}, u32[]{:S(2)}, u32[]{:S(2)}) collective-permute-start(bf16[512,128]{1,0:T(8,128)(2,1)S(1)} %multiply_convert_fusion.1), channel_id=1, source_target_pairs={{1,0},{2,1},{3,2},{4,3},{5,4},{6,5},{7,6},{9,8},{10,9},{11,10},{12... | collective-permute-start | bytes 393224 | tf_op jit(solution)/shard_map/ppermute | solution.py:12
  20.8 8.4 %collective-permute-start.4 = (bf16[512,128]{1,0:T(8,128)(2,1)S(1)}, bf16[512,128]{1,0:T(8,128)(2,1)S(1)}, u32[]{:S(2)}, u32[]{:S(2)}) collective-permute-start(bf16[512,128]{1,0:T(8,128)(2,1)S(1)} %multiply_convert_fusion.1), channel_id=1, source_target_pairs={{2,0},{3,1},{4,2},{5,3},{6,4},{7,5},{10,8},{11,9},{12,10},{13,11},... | collective-permute-start | bytes 393224 | tf_op jit(solution)/shard_map/ppermute | solution.py:12
  25.6 7.6 %collective-permute-start.5 = (bf16[512,128]{1,0:T(8,128)(2,1)S(1)}, bf16[512,128]{1,0:T(8,128)(2,1)S(1)}, u32[]{:S(2)}, u32[]{:S(2)}) collective-permute-start(bf16[512,128]{1,0:T(8,128)(2,1)S(1)} %multiply_convert_fusion.1), channel_id=1, source_target_pairs={{3,0},{4,1},{5,2},{6,3},{7,4},{11,8},{12,9},{13,10},{14,11},{15,12... | collective-permute-start | bytes 393224 | tf_op jit(solution)/shard_map/ppermute | solution.py:12
  82.1 93.6 %copy-start.1 = (f32[1,1,2048]{2,1,0:T(1,128)S(1)}, f32[1,1,2048]{2,1,0:T(1,128)}, u32[]{:S(2)}) copy-start(f32[1,1,2048]{2,1,0:T(1,128)} %param.13) | copy-start | bytes 24580
  269.6 166.1 %copy-start = (f32[512]{0:T(512)S(1)}, f32[512]{0:T(512)}, u32[]{:S(2)}) copy-start(f32[512]{0:T(512)} %param.8) | copy-start | bytes 6148
  363.3 13.3 %collective-permute-start.10 = (f32[512,128]{1,0:T(8,128)S(1)}, f32[512,128]{1,0:T(8,128)S(1)}, u32[]{:S(2)}, u32[]{:S(2)}) collective-permute-start(f32[512,128]{1,0:T(8,128)S(1)} %bitcast.59), channel_id=1, source_target_pairs={{0,2},{1,3},{2,4},{3,5},{4,6},{5,7},{8,10},{9,11},{10,12},{11,13},... | collective-permute-start | bytes 786440 | tf_op jit(solution)/shard_map/ppermute | solution.py:12
  368.7 11.3 %collective-permute-start.11 = (f32[512,128]{1,0:T(8,128)S(1)}, f32[512,128]{1,0:T(8,128)S(1)}, u32[]{:S(2)}, u32[]{:S(2)}) collective-permute-start(f32[512,128]{1,0:T(8,128)S(1)} %bitcast.58), channel_id=1, source_target_pairs={{0,3},{1,4},{2,5},{3,6},{4,7},{8,11},{9,12},{10,13},{11,14},{12,15... | collective-permute-start | bytes 786440 | tf_op jit(solution)/shard_map/ppermute | solution.py:12
  372.6 8.9 %collective-permute-start.6 = (f32[512,128]{1,0:T(8,128)S(1)}, f32[512,128]{1,0:T(8,128)S(1)}, u32[]{:S(2)}, u32[]{:S(2)}) collective-permute-start(f32[512,128]{1,0:T(8,128)S(1)} %bitcast.57), channel_id=1, source_target_pairs={{3,0},{4,1},{5,2},{6,3},{7,4},{11,8},{12,9},{13,10},{14,11},{15,12... | collective-permute-start | bytes 786440 | tf_op jit(solution)/shard_map/ppermute | solution.py:12
  374.0 13.9 %collective-permute-start.7 = (f32[512,128]{1,0:T(8,128)S(1)}, f32[512,128]{1,0:T(8,128)S(1)}, u32[]{:S(2)}, u32[]{:S(2)}) collective-permute-start(f32[512,128]{1,0:T(8,128)S(1)} %bitcast.56), channel_id=1, source_target_pairs={{2,0},{3,1},{4,2},{5,3},{6,4},{7,5},{10,8},{11,9},{12,10},{13,11},... | collective-permute-start | bytes 786440 | tf_op jit(solution)/shard_map/ppermute | solution.py:12
  375.3 12.6 %collective-permute-start.8 = (f32[512,128]{1,0:T(8,128)S(1)}, f32[512,128]{1,0:T(8,128)S(1)}, u32[]{:S(2)}, u32[]{:S(2)}) collective-permute-start(f32[512,128]{1,0:T(8,128)S(1)} %bitcast.55), channel_id=1, source_target_pairs={{1,0},{2,1},{3,2},{4,3},{5,4},{6,5},{7,6},{9,8},{10,9},{11,10},{12... | collective-permute-start | bytes 786440 | tf_op jit(solution)/shard_map/ppermute | solution.py:12
  376.7 11.3 %collective-permute-start.9 = (f32[512,128]{1,0:T(8,128)S(1)}, f32[512,128]{1,0:T(8,128)S(1)}, u32[]{:S(2)}, u32[]{:S(2)}) collective-permute-start(f32[512,128]{1,0:T(8,128)S(1)} %bitcast.54), channel_id=1, source_target_pairs={{0,1},{1,2},{2,3},{3,4},{4,5},{5,6},{6,7},{8,9},{9,10},{10,11},{11... | collective-permute-start | bytes 786440 | tf_op jit(solution)/shard_map/ppermute | solution.py:12
  388.8 103.5 %all-reduce.7.cloned.1.call-start = ((), (), s32[]{:S(2)}) async-start(), calls=%async_computation.1 | async-start | bytes 131072 | tf_op jit(solution)/shard_map/psum | solution.py:57
Sparse Core Ops, SparseCore 0:
  388.9 46.7 all-reduce.4
  438.7 53.5 all-reduce.6
where the time goes:
time: 531 us; the launch traced here: 527 us
  other arithmetic  217 us (41%)
  waiting for transfers between devices  114 us (21%)
  local copies, waits for them, and re-layouts  84.2 us (16%)
  matrix products  64.5 us (12%)
  starting transfers between devices  31.7 us (6%)
  between operations  15 us (3%)
    scatter-add x1, other arithmetic, local(): forward = jax.ops.segment_sum(product, ray_index, num_segments=ray_blocks)  93.6 us
    scatter-add x1, other arithmetic, local(): jax.ops.segment_sum(backward, local_block, num_segments=span_blocks)  93.6 us
    psum x1, waiting for transfers between devices, local(): gram_total = lax.psum(local_gram, 'cell')  54.2 us
    psum x1, waiting for transfers between devices, local(): gradient = lax.psum(owned_rows, 'ray')  46.9 us
    dot_general x1, local copies, waits for them, and re-layouts, local(): jnp.einsum('tij,tik->tjk', tile_set, back_rows, preferred_element_type=jn...  45.8 us
    ppermute x12, starting transfers between devices, passed_along(): return lax.ppermute(value, axis, pairs)  31.6 us
    dot_general x1, matrix products, local(): jnp.einsum('tij,tjk->tik', tile_set, picked, preferred_element_type=jnp.f...  30.6 us
    dot_general x1, matrix products, local(): jnp.einsum('tij,tik->tjk', tile_set, back_rows, preferred_element_type=jn...  29.4 us
  transfers between devices with their start and end apart: 14, of which 6 were waited for; matrix products, arithmetic and copies ran while one was open for 1% of the time, Pallas kernels for 0%

commit v1 on v0

v1 whole, which is shorter than its diff:
```python
import functools
import jax
import jax.numpy as jnp
from jax import lax
from jax.experimental import pallas as pl
from jax.experimental.pallas import tpu as pltpu
from jax.sharding import PartitionSpec as P

REACH = 3


def k2_kernel(group, chunk, ray_ref, cell_ref, count_ref, win_ref, noise_ref, tiles_hbm, out_ref, tiles, fwd, wt, bwd, sems):
    slots, edge = tiles.shape[0], tiles.shape[1]
    nb = noise_ref.shape[0]
    wb = win_ref.shape[0]
    chunks = slots // chunk
    def cp(i):
        s = pl.ds(pl.multiple_of(i * chunk, chunk), chunk)
        return pltpu.make_async_copy(tiles_hbm.at[s], tiles.at[s], sems.at[i])
    @pl.loop(0, chunks)
    def _(i):
        cp(i).start()
    fwd[...] = jnp.zeros_like(fwd)
    bwd[...] = jnp.zeros_like(bwd)
    count = count_ref[0]
    @pl.loop(0, chunks)
    def _(i):
        cp(i).wait()
        @pl.loop(0, chunk // group)
        def _(j):
            t0 = i * chunk + j * group
            prods = []
            for g in range(group):
                t = t0 + g
                prods.append(jnp.dot(tiles[t], win_ref[cell_ref[t]], preferred_element_type=jnp.float32))
            for g in range(group):
                t = t0 + g
                b = jnp.where(t < count, ray_ref[t], nb)
                fwd[b] = fwd[b] + prods[g]
    @pl.loop(0, nb)
    def _(b):
        wt[b] = (fwd[b].T * noise_ref[pl.ds(b, 1), :]).astype(jnp.bfloat16)
    @pl.loop(0, slots // group)
    def _(j):
        t0 = j * group
        prods = []
        for g in range(group):
            t = t0 + g
            prods.append(jnp.dot(wt[ray_ref[t]], tiles[t], preferred_element_type=jnp.float32))
        for g in range(group):
            t = t0 + g
            q = jnp.where(t < count, cell_ref[t], wb)
            bwd[q] = bwd[q] + prods[g]
    @pl.loop(0, wb)
    def _(q):
        out_ref[q] = bwd[q].astype(jnp.bfloat16)

def k2(win, tiles, ray, cell, count, noise, group=48, chunk=48):
    S, E = tiles.shape[0], tiles.shape[1]
    nb, wb = noise.shape[0], win.shape[0]
    V = pl.BlockSpec(memory_space=pltpu.VMEM); M = pl.BlockSpec(memory_space=pltpu.SMEM)
    return pl.pallas_call(functools.partial(k2_kernel, group, chunk),
        out_shape=jax.ShapeDtypeStruct((wb, 128, E), jnp.bfloat16),
        in_specs=[M, M, M, V, V, pl.BlockSpec(memory_space=pl.ANY)], out_specs=V,
        scratch_shapes=[pltpu.VMEM(tiles.shape, jnp.bfloat16), pltpu.VMEM((nb+1, E, 128), jnp.float32),
            pltpu.VMEM((nb, 128, E), jnp.bfloat16), pltpu.VMEM((wb+1, 128, E), jnp.float32), pltpu.SemaphoreType.DMA((S//chunk,))],
        compiler_params=pltpu.CompilerParams(vmem_limit_bytes=48*2**20),
        )(ray, cell, count, win, noise, tiles)


def passed_along(value, axis, by):
    length = lax.axis_size(axis)
    pairs = [(i, i + by) for i in range(length) if 0 <= i + by < length]
    return lax.ppermute(value, axis, pairs)


def summed(value, axis):
    length = lax.axis_size(axis)
    step = 1
    while step < length:
        value = value + lax.ppermute(value, axis, [(i, i ^ step) for i in range(length)])
        step *= 2
    return value


def local(probes, prior, tiles, tile_ray, tile_cell, tile_count, noise):
    edge = tiles.shape[-1]
    width = probes.shape[1]
    own_rows = probes.shape[0]
    own_blocks = own_rows // edge
    owner_total = lax.axis_size("cell")
    owner_index = lax.axis_index("cell")
    span = 2 * REACH + 1
    scaled = (prior[:, None] * probes.astype(jnp.float32)).astype(jnp.bfloat16)
    window = jnp.concatenate(
        [scaled if d == 0 else passed_along(scaled, "cell", -d) for d in range(-REACH, REACH + 1)],
        axis=0,
    ).reshape(span * own_blocks, edge, width)
    local_block = tile_cell[0, 0] - (owner_index - REACH) * own_blocks
    partial = k2(
        window,
        tiles[0, 0],
        tile_ray[0, 0],
        local_block,
        tile_count[0],
        noise[0, 0].reshape(-1, edge),
    ).reshape(span, own_blocks, width, edge)
    own = partial[REACH].astype(jnp.float32)
    for d in range(-REACH, REACH + 1):
        if d != 0:
            own = own + passed_along(partial[REACH + d], "cell", d).astype(jnp.float32)
    root_cells = jnp.sqrt(jnp.float32(own_rows * owner_total))
    gradient = summed(own, "ray")
    sample = prior.reshape(own_blocks, 1, edge) * gradient
    sample = sample.transpose(1, 0, 2).reshape(width, own_rows)
    gram = summed(jnp.dot(sample, sample.T, precision=lax.Precision.HIGHEST), "cell")
    lower = jnp.linalg.cholesky(gram)
    basis = jax.scipy.linalg.solve_triangular(lower, sample, lower=True).T
    return (basis * root_cells, lower.T / root_cells)


def solution(mesh):
    placed = (
        P("cell", None),
        P("cell"),
        P("ray", "cell", None, None, None),
        P("ray", "cell", None),
        P("ray", "cell", None),
        P("ray", "cell"),
        P("ray", "cell", None),
    )
    return jax.shard_map(
        local, mesh=mesh, in_specs=placed, out_specs=(P("cell", None), P()), check_vma=False
    )
```

time: 531 us -> 123 us (0.23)
  other arithmetic: 217 us -> 26.6 us
  waiting for transfers between devices: 114 us -> 30.3 us
  local copies, waits for them, and re-layouts: 84.2 us -> 1.8 us
  matrix products: 64.5 us -> 1.44 us
  Pallas kernels: 0 us -> 23.6 us
  between operations: 15 us -> 1.61 us
    scatter-add x2 -> x0, other arithmetic: 187 us -> none  [the longest x1 93.6 us: local(): forward = jax.ops.segment_sum(product, ray_index, num_segments=ray_blocks)]
    psum x2 -> x0, waiting for transfers between devices: 101 us -> none  [the longest x1 54.2 us: local(): gram_total = lax.psum(local_gram, 'cell')]
    dot_general x3 -> x1, matrix products: 62.4 us -> 0.38 us  [local(): jnp.dot(sample, sample.T, precision=lax.Precision.HIGHEST)]
    dot_general x1 -> x0, local copies, waits for them, and re-layouts: 45.8 us -> none  [local(): jnp.einsum('tij,tik->tjk', tile_set, back_rows, preferred_element_type=jn...]
    gather x2 -> x0, local copies, waits for them, and re-layouts: 36.1 us -> none  [the longest x1 18.1 us: local(): picked = padded[jnp.where(live_slot, local_block, span_blocks)]]
    pallas_call x0 -> x1, Pallas kernels: none -> 23.6 us  [k2(): pl.pallas_call(functools.partial(k2_kernel, group, chunk), out_shape=jax....]
    ppermute x0 -> x5, waiting for transfers between devices: none -> 21.4 us  [summed(): lax.ppermute(value, axis, [(i, i ^ step) for i in range(length)])]
    ppermute x0 -> x5, starting transfers between devices: none -> 6.68 us  [summed(): lax.ppermute(value, axis, [(i, i ^ step) for i in range(length)])]
  transfers between devices with their start and end apart: 14 -> 17, of which waited for: 6 -> 8; matrix products, arithmetic and copies ran while one was open for 1% -> 2% of each run, Pallas kernels for 0% -> 0%
where the time goes in v1:
time: 123 us; the launch traced here: 122 us
  starting transfers between devices  36.7 us (30%)
  waiting for transfers between devices  30.3 us (25%)
  other arithmetic  26.6 us (22%)
  Pallas kernels  23.6 us (19%)
  local copies, waits for them, and re-layouts  1.8 us (1%)
  between operations  1.61 us (1%)
  matrix products  1.44 us (1%)
    ppermute x12, starting transfers between devices, passed_along(): return lax.ppermute(value, axis, pairs)  30 us
    pallas_call x1, Pallas kernels, k2(): pl.pallas_call(functools.partial(k2_kernel, group, chunk), out_shape=jax....  23.6 us
    ppermute x5, waiting for transfers between devices, summed(): lax.ppermute(value, axis, [(i, i ^ step) for i in range(length)])  21.4 us
    another operation x3, other arithmetic, local(): lower = jnp.linalg.cholesky(gram)  12.4 us
    another operation x1, other arithmetic, local(): basis = jax.scipy.linalg.solve_triangular(lower, sample, lower=True).T  9.81 us
    ppermute x12, waiting for transfers between devices, passed_along(): return lax.ppermute(value, axis, pairs)  8.88 us
    ppermute x5, starting transfers between devices, summed(): lax.ppermute(value, axis, [(i, i ^ step) for i in range(length)])  6.68 us
  transfers between devices with their start and end apart: 17, of which 8 were waited for; matrix products, arithmetic and copies ran while one was open for 2% of the time, Pallas kernels for 0%

profile of v1, /device:TPU:0, one launch (start us, length us, event | category | flops | bytes accessed | tf_op | source)
XLA Modules:
  0.0 122.0 jit_solution(858962544996222176)
XLA Ops:
  1.7 4.4 %collective-permute-start = (bf16[512,128]{1,0:T(8,128)(2,1)S(1)}, bf16[512,128]{1,0:T(8,128)(2,1)S(1)}, u32[]{:S(2)}, u32[]{:S(2)}) collective-permute-start(bf16[512,128]{1,0:T(8,128)(2,1)S(1)} %multiply_convert_fusion), channel_id=1, source_target_pairs={{0,3},{1,4},{2,5},{3,6},{4,7},{8,11},{9,12},{10,13},{11,14},{12,15... | collective-permute-start | bytes 393224 | tf_op jit(solution)/shard_map/ppermute | solution.py:74
  6.1 3.5 %collective-permute-start.1 = (bf16[512,128]{1,0:T(8,128)(2,1)S(1)}, bf16[512,128]{1,0:T(8,128)(2,1)S(1)}, u32[]{:S(2)}, u32[]{:S(2)}) collective-permute-start(bf16[512,128]{1,0:T(8,128)(2,1)S(1)} %multiply_convert_fusion), channel_id=1, source_target_pairs={{0,2},{1,3},{2,4},{3,5},{4,6},{5,7},{8,10},{9,11},{10,12},{11,13},... | collective-permute-start | bytes 393224 | tf_op jit(solution)/shard_map/ppermute | solution.py:74
  9.6 3.3 %collective-permute-start.2 = (bf16[512,128]{1,0:T(8,128)(2,1)S(1)}, bf16[512,128]{1,0:T(8,128)(2,1)S(1)}, u32[]{:S(2)}, u32[]{:S(2)}) collective-permute-start(bf16[512,128]{1,0:T(8,128)(2,1)S(1)} %multiply_convert_fusion), channel_id=1, source_target_pairs={{0,1},{1,2},{2,3},{3,4},{4,5},{5,6},{6,7},{8,9},{9,10},{10,11},{11... | collective-permute-start | bytes 393224 | tf_op jit(solution)/shard_map/ppermute | solution.py:74
  12.9 1.3 %collective-permute-start.3 = (bf16[512,128]{1,0:T(8,128)(2,1)S(1)}, bf16[512,128]{1,0:T(8,128)(2,1)S(1)}, u32[]{:S(2)}, u32[]{:S(2)}) collective-permute-start(bf16[512,128]{1,0:T(8,128)(2,1)S(1)} %multiply_convert_fusion), channel_id=1, source_target_pairs={{1,0},{2,1},{3,2},{4,3},{5,4},{6,5},{7,6},{9,8},{10,9},{11,10},{12... | collective-permute-start | bytes 393224 | tf_op jit(solution)/shard_map/ppermute | solution.py:74
  14.2 1.3 %collective-permute-start.4 = (bf16[512,128]{1,0:T(8,128)(2,1)S(1)}, bf16[512,128]{1,0:T(8,128)(2,1)S(1)}, u32[]{:S(2)}, u32[]{:S(2)}) collective-permute-start(bf16[512,128]{1,0:T(8,128)(2,1)S(1)} %multiply_convert_fusion), channel_id=1, source_target_pairs={{2,0},{3,1},{4,2},{5,3},{6,4},{7,5},{10,8},{11,9},{12,10},{13,11},... | collective-permute-start | bytes 393224 | tf_op jit(solution)/shard_map/ppermute | solution.py:74
  17.6 1.3 %collective-permute-start.5 = (bf16[512,128]{1,0:T(8,128)(2,1)S(1)}, bf16[512,128]{1,0:T(8,128)(2,1)S(1)}, u32[]{:S(2)}, u32[]{:S(2)}) collective-permute-start(bf16[512,128]{1,0:T(8,128)(2,1)S(1)} %multiply_convert_fusion), channel_id=1, source_target_pairs={{3,0},{4,1},{5,2},{6,3},{7,4},{11,8},{12,9},{13,10},{14,11},{15,12... | collective-permute-start | bytes 393224 | tf_op jit(solution)/shard_map/ppermute | solution.py:74
  20.1 2.5 %collective-permute-done.4 = bf16[512,128]{1,0:T(8,128)(2,1)S(1)} collective-permute-done((bf16[512,128]{1,0:T(8,128)(2,1)S(1)}, bf16[512,128]{1,0:T(8,128)(2,1)S(1)}, u32[]{:S(2)}, u32[]{:S(2)}) %collective-permute-start.4) | collective-permute-done | bytes 131104 | tf_op jit(solution)/shard_map/ppermute | solution.py:74
  22.6 2.6 %collective-permute-done.5 = bf16[512,128]{1,0:T(8,128)(2,1)S(1)} collective-permute-done((bf16[512,128]{1,0:T(8,128)(2,1)S(1)}, bf16[512,128]{1,0:T(8,128)(2,1)S(1)}, u32[]{:S(2)}, u32[]{:S(2)}) %collective-permute-start.5) | collective-permute-done | bytes 131104 | tf_op jit(solution)/shard_map/ppermute | solution.py:74
  25.9 23.6 %shard_map.86 = bf16[28,128,128]{2,1,0:T(8,128)(2,1)S(1)} custom-call(s32[720]{0:T(1024)S(1)} %reduce.6.ray_ref, s32[720]{0:T(1024)S(1)} %subtract_reduce_fusion.cell_ref, s32[1]{0:T(128)} %bitcast.26.count_ref, bf16[28,128,128]{2,1,0:T(8,128)(2,1)S(1)} %bitcast.27, f32[16,128]{1,0:T(8,128)S(1)} %bitcast.28, bf16[720,128,128]{2,1,0:T(8,128)(2,1)} %bitcast.29), custom_call_target="tpu_custom_call" | custom-call | tf_op jit(solution)/shard_map/pallas_call | solution.py:62
  49.6 5.5 %collective-permute-start.10 = (bf16[4,128,128]{2,1,0:T(8,128)(2,1)S(1)}, bf16[4,128,128]{2,1,0:T(8,128)(2,1)S(1)}, u32[]{:S(2)}, u32[]{:S(2)}) collective-permute-start(bf16[4,128,128]{2,1,0:T(8,128)(2,1)S(1)} %get-tuple-element.8), channel_id=1, source_target_pairs={{0,2},{1,3},{2,4},{3,5},{4,6},{5,7},{8,10},{9,11},{10,12},{11,13},... | collective-permute-start | bytes 393224 | tf_op jit(solution)/shard_map/ppermute | solution.py:74
  55.1 2.4 %collective-permute-start.11 = (bf16[4,128,128]{2,1,0:T(8,128)(2,1)S(1)}, bf16[4,128,128]{2,1,0:T(8,128)(2,1)S(1)}, u32[]{:S(2)}, u32[]{:S(2)}) collective-permute-start(bf16[4,128,128]{2,1,0:T(8,128)(2,1)S(1)} %get-tuple-element.7), channel_id=1, source_target_pairs={{0,3},{1,4},{2,5},{3,6},{4,7},{8,11},{9,12},{10,13},{11,14},{12,15... | collective-permute-start | bytes 393224 | tf_op jit(solution)/shard_map/ppermute | solution.py:74
  57.5 1.3 %collective-permute-start.6 = (bf16[4,128,128]{2,1,0:T(8,128)(2,1)S(1)}, bf16[4,128,128]{2,1,0:T(8,128)(2,1)S(1)}, u32[]{:S(2)}, u32[]{:S(2)}) collective-permute-start(bf16[4,128,128]{2,1,0:T(8,128)(2,1)S(1)} %get-tuple-element.6), channel_id=1, source_target_pairs={{3,0},{4,1},{5,2},{6,3},{7,4},{11,8},{12,9},{13,10},{14,11},{15,12... | collective-permute-start | bytes 393224 | tf_op jit(solution)/shard_map/ppermute | solution.py:74
  61.4 3.2 %collective-permute-start.9 = (bf16[4,128,128]{2,1,0:T(8,128)(2,1)S(1)}, bf16[4,128,128]{2,1,0:T(8,128)(2,1)S(1)}, u32[]{:S(2)}, u32[]{:S(2)}) collective-permute-start(bf16[4,128,128]{2,1,0:T(8,128)(2,1)S(1)} %get-tuple-element.9), channel_id=1, source_target_pairs={{0,1},{1,2},{2,3},{3,4},{4,5},{5,6},{6,7},{8,9},{9,10},{10,11},{11... | collective-permute-start | bytes 393224 | tf_op jit(solution)/shard_map/ppermute | solution.py:74
  64.6 3.7 %collective-permute-done.7 = bf16[4,128,128]{2,1,0:T(8,128)(2,1)S(1)} collective-permute-done((bf16[4,128,128]{2,1,0:T(8,128)(2,1)S(1)}, bf16[4,128,128]{2,1,0:T(8,128)(2,1)S(1)}, u32[]{:S(2)}, u32[]{:S(2)}) %collective-permute-start.7) | collective-permute-done | bytes 131104 | tf_op jit(solution)/shard_map/ppermute | solution.py:74
  68.5 1.6 %collective-permute-start.12 = (f32[4,128,128]{2,1,0:T(8,128)S(1)}, f32[4,128,128]{2,1,0:T(8,128)S(1)}, u32[]{:S(2)}, u32[]{:S(2)}) collective-permute-start(f32[4,128,128]{2,1,0:T(8,128)S(1)} %convert_add_fusion), channel_id=1, source_target_pairs={{0,8},{8,0},{16,24},{24,16},{1,9},{9,1},{17,25},{25,17},{2,10},{10... | collective-permute-start | bytes 786440 | tf_op jit(solution)/shard_map/ppermute | solution.py:81
  70.1 7.4 %collective-permute-done.12 = f32[4,128,128]{2,1,0:T(8,128)S(1)} collective-permute-done((f32[4,128,128]{2,1,0:T(8,128)S(1)}, f32[4,128,128]{2,1,0:T(8,128)S(1)}, u32[]{:S(2)}, u32[]{:S(2)}) %collective-permute-start.12) | collective-permute-done | bytes 262176 | tf_op jit(solution)/shard_map/ppermute | solution.py:81
  77.5 1.6 %collective-permute-start.13 = (f32[4,128,128]{2,1,0:T(8,128)S(1)}, f32[4,128,128]{2,1,0:T(8,128)S(1)}, u32[]{:S(2)}, u32[]{:S(2)}) collective-permute-start(f32[4,128,128]{2,1,0:T(8,128)S(1)} %add.52), channel_id=1, source_target_pairs={{0,16},{8,24},{16,0},{24,8},{1,17},{9,25},{17,1},{25,9},{2,18},{10... | collective-permute-start | bytes 786440 | tf_op jit(solution)/shard_map/ppermute | solution.py:81
  79.1 6.8 %collective-permute-done.13 = f32[4,128,128]{2,1,0:T(8,128)S(1)} collective-permute-done((f32[4,128,128]{2,1,0:T(8,128)S(1)}, f32[4,128,128]{2,1,0:T(8,128)S(1)}, u32[]{:S(2)}, u32[]{:S(2)}) %collective-permute-start.13) | collective-permute-done | bytes 262176 | tf_op jit(solution)/shard_map/ppermute | solution.py:81
  87.7 1.4 %collective-permute-start.15 = (f32[128,128]{0,1:T(8,128)S(1)}, f32[128,128]{0,1:T(8,128)S(1)}, u32[]{:S(2)}, u32[]{:S(2)}) collective-permute-start(f32[128,128]{0,1:T(8,128)S(1)} %add.54), channel_id=1, source_target_pairs={{0,2},{1,3},{2,0},{3,1},{4,6},{5,7},{6,4},{7,5},{8,10},{9,11},{10,... | collective-permute-start | bytes 196616 | tf_op jit(solution)/shard_map/ppermute | solution.py:81
  89.0 3.0 %collective-permute-done.15 = f32[128,128]{0,1:T(8,128)S(1)} collective-permute-done((f32[128,128]{0,1:T(8,128)S(1)}, f32[128,128]{0,1:T(8,128)S(1)}, u32[]{:S(2)}, u32[]{:S(2)}) %collective-permute-start.15) | collective-permute-done | bytes 65568 | tf_op jit(solution)/shard_map/ppermute | solution.py:81
  92.0 2.1 %collective-permute-start.16 = (f32[128,128]{0,1:T(8,128)S(1)}, f32[128,128]{0,1:T(8,128)S(1)}, u32[]{:S(2)}, u32[]{:S(2)}) collective-permute-start(f32[128,128]{0,1:T(8,128)S(1)} %add.55), channel_id=1, source_target_pairs={{0,4},{1,5},{2,6},{3,7},{4,0},{5,1},{6,2},{7,3},{8,12},{9,13},{10,... | collective-permute-start | bytes 196616 | tf_op jit(solution)/shard_map/ppermute | solution.py:81
  94.3 3.0 %collective-permute-done.16 = f32[128,128]{0,1:T(8,128)S(1)} collective-permute-done((f32[128,128]{0,1:T(8,128)S(1)}, f32[128,128]{0,1:T(8,128)S(1)}, u32[]{:S(2)}, u32[]{:S(2)}) %collective-permute-start.16) | collective-permute-done | bytes 65568 | tf_op jit(solution)/shard_map/ppermute | solution.py:81
  97.4 11.7 %cholesky.16 = f32[128,128]{1,0:T(8,128)S(1)} custom-call(f32[128,128]{1,0:T(8,128)S(1)} %fusion.1), custom_call_target="Cholesky" | custom-call | tf_op jit(solution)/shard_map/jit(cholesky)/cholesky | solution.py:117
  110.4 9.8 %custom-call.7 = f32[1,128,128]{1,2,0:T(8,128)S(1)} custom-call(f32[1,128,128]{2,1,0:T(8,128)S(1)} %get-tuple-element.13), custom_call_target="InvertDiagBlocksLowerTriangular" | custom-call | tf_op jit(solution)/shard_map/jit(_solve_triangular)/triangular_solve | solution.py:118
  (43 shorter events, 12.2 us)
Async XLA Ops:
  0.6 85.3 %copy-start.1 = (f32[512]{0:T(512)S(1)}, f32[512]{0:T(512)}, u32[]{:S(2)}) copy-start(f32[512]{0:T(512)} %param.8) | copy-start | bytes 6148
  1.7 15.9 %collective-permute-start = (bf16[512,128]{1,0:T(8,128)(2,1)S(1)}, bf16[512,128]{1,0:T(8,128)(2,1)S(1)}, u32[]{:S(2)}, u32[]{:S(2)}) collective-permute-start(bf16[512,128]{1,0:T(8,128)(2,1)S(1)} %multiply_convert_fusion), channel_id=1, source_target_pairs={{0,3},{1,4},{2,5},{3,6},{4,7},{8,11},{9,12},{10,13},{11,14},{12,15... | collective-permute-start | bytes 393224 | tf_op jit(solution)/shard_map/ppermute | solution.py:74
  6.1 12.8 %collective-permute-start.1 = (bf16[512,128]{1,0:T(8,128)(2,1)S(1)}, bf16[512,128]{1,0:T(8,128)(2,1)S(1)}, u32[]{:S(2)}, u32[]{:S(2)}) collective-permute-start(bf16[512,128]{1,0:T(8,128)(2,1)S(1)} %multiply_convert_fusion), channel_id=1, source_target_pairs={{0,2},{1,3},{2,4},{3,5},{4,6},{5,7},{8,10},{9,11},{10,12},{11,13},... | collective-permute-start | bytes 393224 | tf_op jit(solution)/shard_map/ppermute | solution.py:74
  9.6 9.4 %collective-permute-start.2 = (bf16[512,128]{1,0:T(8,128)(2,1)S(1)}, bf16[512,128]{1,0:T(8,128)(2,1)S(1)}, u32[]{:S(2)}, u32[]{:S(2)}) collective-permute-start(bf16[512,128]{1,0:T(8,128)(2,1)S(1)} %multiply_convert_fusion), channel_id=1, source_target_pairs={{0,1},{1,2},{2,3},{3,4},{4,5},{5,6},{6,7},{8,9},{9,10},{10,11},{11... | collective-permute-start | bytes 393224 | tf_op jit(solution)/shard_map/ppermute | solution.py:74
  12.9 7.1 %collective-permute-start.3 = (bf16[512,128]{1,0:T(8,128)(2,1)S(1)}, bf16[512,128]{1,0:T(8,128)(2,1)S(1)}, u32[]{:S(2)}, u32[]{:S(2)}) collective-permute-start(bf16[512,128]{1,0:T(8,128)(2,1)S(1)} %multiply_convert_fusion), channel_id=1, source_target_pairs={{1,0},{2,1},{3,2},{4,3},{5,4},{6,5},{7,6},{9,8},{10,9},{11,10},{12... | collective-permute-start | bytes 393224 | tf_op jit(solution)/shard_map/ppermute | solution.py:74
  14.2 8.4 %collective-permute-start.4 = (bf16[512,128]{1,0:T(8,128)(2,1)S(1)}, bf16[512,128]{1,0:T(8,128)(2,1)S(1)}, u32[]{:S(2)}, u32[]{:S(2)}) collective-permute-start(bf16[512,128]{1,0:T(8,128)(2,1)S(1)} %multiply_convert_fusion), channel_id=1, source_target_pairs={{2,0},{3,1},{4,2},{5,3},{6,4},{7,5},{10,8},{11,9},{12,10},{13,11},... | collective-permute-start | bytes 393224 | tf_op jit(solution)/shard_map/ppermute | solution.py:74
  17.6 7.6 %collective-permute-start.5 = (bf16[512,128]{1,0:T(8,128)(2,1)S(1)}, bf16[512,128]{1,0:T(8,128)(2,1)S(1)}, u32[]{:S(2)}, u32[]{:S(2)}) collective-permute-start(bf16[512,128]{1,0:T(8,128)(2,1)S(1)} %multiply_convert_fusion), channel_id=1, source_target_pairs={{3,0},{4,1},{5,2},{6,3},{7,4},{11,8},{12,9},{13,10},{14,11},{15,12... | collective-permute-start | bytes 393224 | tf_op jit(solution)/shard_map/ppermute | solution.py:74
  25.2 0.7 copy-start
  49.6 11.8 %collective-permute-start.10 = (bf16[4,128,128]{2,1,0:T(8,128)(2,1)S(1)}, bf16[4,128,128]{2,1,0:T(8,128)(2,1)S(1)}, u32[]{:S(2)}, u32[]{:S(2)}) collective-permute-start(bf16[4,128,128]{2,1,0:T(8,128)(2,1)S(1)} %get-tuple-element.8), channel_id=1, source_target_pairs={{0,2},{1,3},{2,4},{3,5},{4,6},{5,7},{8,10},{9,11},{10,12},{11,13},... | collective-permute-start | bytes 393224 | tf_op jit(solution)/shard_map/ppermute | solution.py:74
  55.1 9.5 %collective-permute-start.11 = (bf16[4,128,128]{2,1,0:T(8,128)(2,1)S(1)}, bf16[4,128,128]{2,1,0:T(8,128)(2,1)S(1)}, u32[]{:S(2)}, u32[]{:S(2)}) collective-permute-start(bf16[4,128,128]{2,1,0:T(8,128)(2,1)S(1)} %get-tuple-element.7), channel_id=1, source_target_pairs={{0,3},{1,4},{2,5},{3,6},{4,7},{8,11},{9,12},{10,13},{11,14},{12,15... | collective-permute-start | bytes 393224 | tf_op jit(solution)/shard_map/ppermute | solution.py:74
  57.5 7.2 %collective-permute-start.6 = (bf16[4,128,128]{2,1,0:T(8,128)(2,1)S(1)}, bf16[4,128,128]{2,1,0:T(8,128)(2,1)S(1)}, u32[]{:S(2)}, u32[]{:S(2)}) collective-permute-start(bf16[4,128,128]{2,1,0:T(8,128)(2,1)S(1)} %get-tuple-element.6), channel_id=1, source_target_pairs={{3,0},{4,1},{5,2},{6,3},{7,4},{11,8},{12,9},{13,10},{14,11},{15,12... | collective-permute-start | bytes 393224 | tf_op jit(solution)/shard_map/ppermute | solution.py:74
  58.8 9.6 %collective-permute-start.7 = (bf16[4,128,128]{2,1,0:T(8,128)(2,1)S(1)}, bf16[4,128,128]{2,1,0:T(8,128)(2,1)S(1)}, u32[]{:S(2)}, u32[]{:S(2)}) collective-permute-start(bf16[4,128,128]{2,1,0:T(8,128)(2,1)S(1)} %get-tuple-element.11), channel_id=1, source_target_pairs={{2,0},{3,1},{4,2},{5,3},{6,4},{7,5},{10,8},{11,9},{12,10},{13,11},... | collective-permute-start | bytes 393224 | tf_op jit(solution)/shard_map/ppermute | solution.py:74
  60.1 8.3 %collective-permute-start.8 = (bf16[4,128,128]{2,1,0:T(8,128)(2,1)S(1)}, bf16[4,128,128]{2,1,0:T(8,128)(2,1)S(1)}, u32[]{:S(2)}, u32[]{:S(2)}) collective-permute-start(bf16[4,128,128]{2,1,0:T(8,128)(2,1)S(1)} %get-tuple-element.10), channel_id=1, source_target_pairs={{1,0},{2,1},{3,2},{4,3},{5,4},{6,5},{7,6},{9,8},{10,9},{11,10},{12... | collective-permute-start | bytes 393224 | tf_op jit(solution)/shard_map/ppermute | solution.py:74
  61.4 7.0 %collective-permute-start.9 = (bf16[4,128,128]{2,1,0:T(8,128)(2,1)S(1)}, bf16[4,128,128]{2,1,0:T(8,128)(2,1)S(1)}, u32[]{:S(2)}, u32[]{:S(2)}) collective-permute-start(bf16[4,128,128]{2,1,0:T(8,128)(2,1)S(1)} %get-tuple-element.9), channel_id=1, source_target_pairs={{0,1},{1,2},{2,3},{3,4},{4,5},{5,6},{6,7},{8,9},{9,10},{10,11},{11... | collective-permute-start | bytes 393224 | tf_op jit(solution)/shard_map/ppermute | solution.py:74
  68.5 9.0 %collective-permute-start.12 = (f32[4,128,128]{2,1,0:T(8,128)S(1)}, f32[4,128,128]{2,1,0:T(8,128)S(1)}, u32[]{:S(2)}, u32[]{:S(2)}) collective-permute-start(f32[4,128,128]{2,1,0:T(8,128)S(1)} %convert_add_fusion), channel_id=1, source_target_pairs={{0,8},{8,0},{16,24},{24,16},{1,9},{9,1},{17,25},{25,17},{2,10},{10... | collective-permute-start | bytes 786440 | tf_op jit(solution)/shard_map/ppermute | solution.py:81
  77.5 8.4 %collective-permute-start.13 = (f32[4,128,128]{2,1,0:T(8,128)S(1)}, f32[4,128,128]{2,1,0:T(8,128)S(1)}, u32[]{:S(2)}, u32[]{:S(2)}) collective-permute-start(f32[4,128,128]{2,1,0:T(8,128)S(1)} %add.52), channel_id=1, source_target_pairs={{0,16},{8,24},{16,0},{24,8},{1,17},{9,25},{17,1},{25,9},{2,18},{10... | collective-permute-start | bytes 786440 | tf_op jit(solution)/shard_map/ppermute | solution.py:81
  86.3 1.3 %collective-permute-start.14 = (f32[128,128]{0,1:T(8,128)S(1)}, f32[128,128]{0,1:T(8,128)S(1)}, u32[]{:S(2)}, u32[]{:S(2)}) collective-permute-start(f32[128,128]{0,1:T(8,128)S(1)} %convolution_bitcast_fusion), channel_id=1, source_target_pairs={{0,1},{1,0},{2,3},{3,2},{4,5},{5,4},{6,7},{7,6},{8,9},{9,8},{10,11... | collective-permute-start | bytes 196616 | tf_op jit(solution)/shard_map/ppermute | solution.py:81
  87.7 4.3 %collective-permute-start.15 = (f32[128,128]{0,1:T(8,128)S(1)}, f32[128,128]{0,1:T(8,128)S(1)}, u32[]{:S(2)}, u32[]{:S(2)}) collective-permute-start(f32[128,128]{0,1:T(8,128)S(1)} %add.54), channel_id=1, source_target_pairs={{0,2},{1,3},{2,0},{3,1},{4,6},{5,7},{6,4},{7,5},{8,10},{9,11},{10,... | collective-permute-start | bytes 196616 | tf_op jit(solution)/shard_map/ppermute | solution.py:81
  92.0 5.2 %collective-permute-start.16 = (f32[128,128]{0,1:T(8,128)S(1)}, f32[128,128]{0,1:T(8,128)S(1)}, u32[]{:S(2)}, u32[]{:S(2)}) collective-permute-start(f32[128,128]{0,1:T(8,128)S(1)} %add.55), channel_id=1, source_target_pairs={{0,4},{1,5},{2,6},{3,7},{4,0},{5,1},{6,2},{7,3},{8,12},{9,13},{10,... | collective-permute-start | bytes 196616 | tf_op jit(solution)/shard_map/ppermute | solution.py:81

commit v2 on v1

--- a/solution.py
+++ b/solution.py
@@ -55,7 +55,7 @@
     def _(q):
         out_ref[q] = bwd[q].astype(jnp.bfloat16)
 
-def k2(win, tiles, ray, cell, count, noise, group=48, chunk=48):
+def k2(win, tiles, ray, cell, count, noise, group=72, chunk=72):
     S, E = tiles.shape[0], tiles.shape[1]
     nb, wb = noise.shape[0], win.shape[0]
     V = pl.BlockSpec(memory_space=pltpu.VMEM); M = pl.BlockSpec(memory_space=pltpu.SMEM)
@@ -74,11 +74,13 @@
     return lax.ppermute(value, axis, pairs)
 
 
-def summed(value, axis):
+def summed(value, axis, kind=jnp.float32):
     length = lax.axis_size(axis)
     step = 1
     while step < length:
-        value = value + lax.ppermute(value, axis, [(i, i ^ step) for i in range(length)])
+        sent = value.astype(kind)
+        got = lax.ppermute(sent, axis, [(i, i ^ step) for i in range(length)])
+        value = sent.astype(jnp.float32) + got.astype(jnp.float32)
         step *= 2
     return value
 
@@ -110,7 +112,7 @@
         if d != 0:
             own = own + passed_along(partial[REACH + d], "cell", d).astype(jnp.float32)
     root_cells = jnp.sqrt(jnp.float32(own_rows * owner_total))
-    gradient = summed(own, "ray")
+    gradient = summed(own, "ray", jnp.bfloat16)
     sample = prior.reshape(own_blocks, 1, edge) * gradient
     sample = sample.transpose(1, 0, 2).reshape(width, own_rows)
     gram = summed(jnp.dot(sample, sample.T, precision=lax.Precision.HIGHEST), "cell")

time: 123 us -> 116 us (0.943)
  waiting for transfers between devices: 30.3 us -> 23.9 us
    ppermute x5, waiting for transfers between devices: 21.4 us -> 15 us  [summed(): got = lax.ppermute(sent, axis, [(i, i ^ step) for i in range(length)])]
where the time goes in v2:
time: 116 us
  starting transfers between devices  37.8 us (33%)
  other arithmetic  26.6 us (23%)
  waiting for transfers between devices  23.9 us (21%)
  Pallas kernels  22.5 us (19%)
  local copies, waits for them, and re-layouts  1.8 us (2%)
  between operations  1.61 us (1%)
  matrix products  1.44 us (1%)
    ppermute x12, starting transfers between devices, passed_along(): return lax.ppermute(value, axis, pairs)  30.1 us
    pallas_call x1, Pallas kernels, k2(): pl.pallas_call(functools.partial(k2_kernel, group, chunk), out_shape=jax....  22.5 us
    ppermute x5, waiting for transfers between devices, summed(): got = lax.ppermute(sent, axis, [(i, i ^ step) for i in range(length)])  15 us
    another operation x3, other arithmetic, local(): lower = jnp.linalg.cholesky(gram)  12.4 us
    another operation x1, other arithmetic, local(): basis = jax.scipy.linalg.solve_triangular(lower, sample, lower=True).T  9.81 us
    ppermute x12, waiting for transfers between devices, passed_along(): return lax.ppermute(value, axis, pairs)  8.87 us
    ppermute x5, starting transfers between devices, summed(): got = lax.ppermute(sent, axis, [(i, i ^ step) for i in range(length)])  7.73 us
  transfers between devices with their start and end apart: 17, of which 8 were waited for; matrix products, arithmetic and copies ran while one was open for 2% of the time, Pallas kernels for 0%

profile of v2, /device:TPU:0, one launch (start us, length us, event | category | flops | bytes accessed | tf_op | source)
XLA Modules:
  0.0 115.7 jit_solution(2321941294844185503)
XLA Ops:
  1.7 4.4 %collective-permute-start = (bf16[512,128]{1,0:T(8,128)(2,1)S(1)}, bf16[512,128]{1,0:T(8,128)(2,1)S(1)}, u32[]{:S(2)}, u32[]{:S(2)}) collective-permute-start(bf16[512,128]{1,0:T(8,128)(2,1)S(1)} %multiply_convert_fusion), channel_id=1, source_target_pairs={{0,3},{1,4},{2,5},{3,6},{4,7},{8,11},{9,12},{10,13},{11,14},{12,15... | collective-permute-start | bytes 393224 | tf_op jit(solution)/shard_map/ppermute | solution.py:74
  6.1 3.5 %collective-permute-start.1 = (bf16[512,128]{1,0:T(8,128)(2,1)S(1)}, bf16[512,128]{1,0:T(8,128)(2,1)S(1)}, u32[]{:S(2)}, u32[]{:S(2)}) collective-permute-start(bf16[512,128]{1,0:T(8,128)(2,1)S(1)} %multiply_convert_fusion), channel_id=1, source_target_pairs={{0,2},{1,3},{2,4},{3,5},{4,6},{5,7},{8,10},{9,11},{10,12},{11,13},... | collective-permute-start | bytes 393224 | tf_op jit(solution)/shard_map/ppermute | solution.py:74
  9.6 3.3 %collective-permute-start.2 = (bf16[512,128]{1,0:T(8,128)(2,1)S(1)}, bf16[512,128]{1,0:T(8,128)(2,1)S(1)}, u32[]{:S(2)}, u32[]{:S(2)}) collective-permute-start(bf16[512,128]{1,0:T(8,128)(2,1)S(1)} %multiply_convert_fusion), channel_id=1, source_target_pairs={{0,1},{1,2},{2,3},{3,4},{4,5},{5,6},{6,7},{8,9},{9,10},{10,11},{11... | collective-permute-start | bytes 393224 | tf_op jit(solution)/shard_map/ppermute | solution.py:74
  12.9 1.3 %collective-permute-start.3 = (bf16[512,128]{1,0:T(8,128)(2,1)S(1)}, bf16[512,128]{1,0:T(8,128)(2,1)S(1)}, u32[]{:S(2)}, u32[]{:S(2)}) collective-permute-start(bf16[512,128]{1,0:T(8,128)(2,1)S(1)} %multiply_convert_fusion), channel_id=1, source_target_pairs={{1,0},{2,1},{3,2},{4,3},{5,4},{6,5},{7,6},{9,8},{10,9},{11,10},{12... | collective-permute-start | bytes 393224 | tf_op jit(solution)/shard_map/ppermute | solution.py:74
  14.2 1.3 %collective-permute-start.4 = (bf16[512,128]{1,0:T(8,128)(2,1)S(1)}, bf16[512,128]{1,0:T(8,128)(2,1)S(1)}, u32[]{:S(2)}, u32[]{:S(2)}) collective-permute-start(bf16[512,128]{1,0:T(8,128)(2,1)S(1)} %multiply_convert_fusion), channel_id=1, source_target_pairs={{2,0},{3,1},{4,2},{5,3},{6,4},{7,5},{10,8},{11,9},{12,10},{13,11},... | collective-permute-start | bytes 393224 | tf_op jit(solution)/shard_map/ppermute | solution.py:74
  17.6 1.3 %collective-permute-start.5 = (bf16[512,128]{1,0:T(8,128)(2,1)S(1)}, bf16[512,128]{1,0:T(8,128)(2,1)S(1)}, u32[]{:S(2)}, u32[]{:S(2)}) collective-permute-start(bf16[512,128]{1,0:T(8,128)(2,1)S(1)} %multiply_convert_fusion), channel_id=1, source_target_pairs={{3,0},{4,1},{5,2},{6,3},{7,4},{11,8},{12,9},{13,10},{14,11},{15,12... | collective-permute-start | bytes 393224 | tf_op jit(solution)/shard_map/ppermute | solution.py:74
  20.1 2.5 %collective-permute-done.4 = bf16[512,128]{1,0:T(8,128)(2,1)S(1)} collective-permute-done((bf16[512,128]{1,0:T(8,128)(2,1)S(1)}, bf16[512,128]{1,0:T(8,128)(2,1)S(1)}, u32[]{:S(2)}, u32[]{:S(2)}) %collective-permute-start.4) | collective-permute-done | bytes 131104 | tf_op jit(solution)/shard_map/ppermute | solution.py:74
  22.6 2.6 %collective-permute-done.5 = bf16[512,128]{1,0:T(8,128)(2,1)S(1)} collective-permute-done((bf16[512,128]{1,0:T(8,128)(2,1)S(1)}, bf16[512,128]{1,0:T(8,128)(2,1)S(1)}, u32[]{:S(2)}, u32[]{:S(2)}) %collective-permute-start.5) | collective-permute-done | bytes 131104 | tf_op jit(solution)/shard_map/ppermute | solution.py:74
  25.9 22.5 %shard_map.86 = bf16[28,128,128]{2,1,0:T(8,128)(2,1)S(1)} custom-call(s32[720]{0:T(1024)S(1)} %reduce.6.ray_ref, s32[720]{0:T(1024)S(1)} %subtract_reduce_fusion.cell_ref, s32[1]{0:T(128)} %bitcast.26.count_ref, bf16[28,128,128]{2,1,0:T(8,128)(2,1)S(1)} %bitcast.27, f32[16,128]{1,0:T(8,128)S(1)} %bitcast.28, bf16[720,128,128]{2,1,0:T(8,128)(2,1)} %bitcast.29), custom_call_target="tpu_custom_call" | custom-call | tf_op jit(solution)/shard_map/pallas_call | solution.py:62
  48.5 5.5 %collective-permute-start.10 = (bf16[4,128,128]{2,1,0:T(8,128)(2,1)S(1)}, bf16[4,128,128]{2,1,0:T(8,128)(2,1)S(1)}, u32[]{:S(2)}, u32[]{:S(2)}) collective-permute-start(bf16[4,128,128]{2,1,0:T(8,128)(2,1)S(1)} %get-tuple-element.8), channel_id=1, source_target_pairs={{0,2},{1,3},{2,4},{3,5},{4,6},{5,7},{8,10},{9,11},{10,12},{11,13},... | collective-permute-start | bytes 393224 | tf_op jit(solution)/shard_map/ppermute | solution.py:74
  54.0 2.4 %collective-permute-start.11 = (bf16[4,128,128]{2,1,0:T(8,128)(2,1)S(1)}, bf16[4,128,128]{2,1,0:T(8,128)(2,1)S(1)}, u32[]{:S(2)}, u32[]{:S(2)}) collective-permute-start(bf16[4,128,128]{2,1,0:T(8,128)(2,1)S(1)} %get-tuple-element.7), channel_id=1, source_target_pairs={{0,3},{1,4},{2,5},{3,6},{4,7},{8,11},{9,12},{10,13},{11,14},{12,15... | collective-permute-start | bytes 393224 | tf_op jit(solution)/shard_map/ppermute | solution.py:74
  56.4 1.3 %collective-permute-start.6 = (bf16[4,128,128]{2,1,0:T(8,128)(2,1)S(1)}, bf16[4,128,128]{2,1,0:T(8,128)(2,1)S(1)}, u32[]{:S(2)}, u32[]{:S(2)}) collective-permute-start(bf16[4,128,128]{2,1,0:T(8,128)(2,1)S(1)} %get-tuple-element.6), channel_id=1, source_target_pairs={{3,0},{4,1},{5,2},{6,3},{7,4},{11,8},{12,9},{13,10},{14,11},{15,12... | collective-permute-start | bytes 393224 | tf_op jit(solution)/shard_map/ppermute | solution.py:74
  60.3 3.3 %collective-permute-start.9 = (bf16[4,128,128]{2,1,0:T(8,128)(2,1)S(1)}, bf16[4,128,128]{2,1,0:T(8,128)(2,1)S(1)}, u32[]{:S(2)}, u32[]{:S(2)}) collective-permute-start(bf16[4,128,128]{2,1,0:T(8,128)(2,1)S(1)} %get-tuple-element.9), channel_id=1, source_target_pairs={{0,1},{1,2},{2,3},{3,4},{4,5},{5,6},{6,7},{8,9},{9,10},{10,11},{11... | collective-permute-start | bytes 393224 | tf_op jit(solution)/shard_map/ppermute | solution.py:74
  63.6 3.7 %collective-permute-done.7 = bf16[4,128,128]{2,1,0:T(8,128)(2,1)S(1)} collective-permute-done((bf16[4,128,128]{2,1,0:T(8,128)(2,1)S(1)}, bf16[4,128,128]{2,1,0:T(8,128)(2,1)S(1)}, u32[]{:S(2)}, u32[]{:S(2)}) %collective-permute-start.7) | collective-permute-done | bytes 131104 | tf_op jit(solution)/shard_map/ppermute | solution.py:74
  67.5 1.5 %collective-permute-start.12 = (bf16[4,128,128]{2,1,0:T(8,128)(2,1)S(1)}, bf16[4,128,128]{2,1,0:T(8,128)(2,1)S(1)}, u32[]{:S(2)}, u32[]{:S(2)}) collective-permute-start(bf16[4,128,128]{2,1,0:T(8,128)(2,1)S(1)} %add_convert_fusion.1), channel_id=1, source_target_pairs={{0,8},{8,0},{16,24},{24,16},{1,9},{9,1},{17,25},{25,17},{2,10},{10... | collective-permute-start | bytes 393224 | tf_op jit(solution)/shard_map/ppermute | solution.py:82
  69.0 4.6 %collective-permute-done.12 = bf16[4,128,128]{2,1,0:T(8,128)(2,1)S(1)} collective-permute-done((bf16[4,128,128]{2,1,0:T(8,128)(2,1)S(1)}, bf16[4,128,128]{2,1,0:T(8,128)(2,1)S(1)}, u32[]{:S(2)}, u32[]{:S(2)}) %collective-permute-start.12) | collective-permute-done | bytes 131104 | tf_op jit(solution)/shard_map/ppermute | solution.py:82
  73.7 1.6 %collective-permute-start.13 = (bf16[4,128,128]{2,1,0:T(8,128)(2,1)S(1)}, bf16[4,128,128]{2,1,0:T(8,128)(2,1)S(1)}, u32[]{:S(2)}, u32[]{:S(2)}) collective-permute-start(bf16[4,128,128]{2,1,0:T(8,128)(2,1)S(1)} %add_convert_fusion), channel_id=1, source_target_pairs={{0,16},{8,24},{16,0},{24,8},{1,17},{9,25},{17,1},{25,9},{2,18},{10... | collective-permute-start | bytes 393224 | tf_op jit(solution)/shard_map/ppermute | solution.py:82
  75.3 4.0 %collective-permute-done.13 = bf16[4,128,128]{2,1,0:T(8,128)(2,1)S(1)} collective-permute-done((bf16[4,128,128]{2,1,0:T(8,128)(2,1)S(1)}, bf16[4,128,128]{2,1,0:T(8,128)(2,1)S(1)}, u32[]{:S(2)}, u32[]{:S(2)}) %collective-permute-start.13) | collective-permute-done | bytes 131104 | tf_op jit(solution)/shard_map/ppermute | solution.py:82
  81.0 1.6 %collective-permute-start.15 = (f32[128,128]{0,1:T(8,128)S(1)}, f32[128,128]{0,1:T(8,128)S(1)}, u32[]{:S(2)}, u32[]{:S(2)}) collective-permute-start(f32[128,128]{0,1:T(8,128)S(1)} %add.54), channel_id=1, source_target_pairs={{0,2},{1,3},{2,0},{3,1},{4,6},{5,7},{6,4},{7,5},{8,10},{9,11},{10,... | collective-permute-start | bytes 196616 | tf_op jit(solution)/shard_map/ppermute | solution.py:82
  82.6 2.8 %collective-permute-done.15 = f32[128,128]{0,1:T(8,128)S(1)} collective-permute-done((f32[128,128]{0,1:T(8,128)S(1)}, f32[128,128]{0,1:T(8,128)S(1)}, u32[]{:S(2)}, u32[]{:S(2)}) %collective-permute-start.15) | collective-permute-done | bytes 65568 | tf_op jit(solution)/shard_map/ppermute | solution.py:82
  85.4 3.0 %collective-permute-start.16 = (f32[128,128]{0,1:T(8,128)S(1)}, f32[128,128]{0,1:T(8,128)S(1)}, u32[]{:S(2)}, u32[]{:S(2)}) collective-permute-start(f32[128,128]{0,1:T(8,128)S(1)} %add.55), channel_id=1, source_target_pairs={{0,4},{1,5},{2,6},{3,7},{4,0},{5,1},{6,2},{7,3},{8,12},{9,13},{10,... | collective-permute-start | bytes 196616 | tf_op jit(solution)/shard_map/ppermute | solution.py:82
  88.5 2.4 %collective-permute-done.16 = f32[128,128]{0,1:T(8,128)S(1)} collective-permute-done((f32[128,128]{0,1:T(8,128)S(1)}, f32[128,128]{0,1:T(8,128)S(1)}, u32[]{:S(2)}, u32[]{:S(2)}) %collective-permute-start.16) | collective-permute-done | bytes 65568 | tf_op jit(solution)/shard_map/ppermute | solution.py:82
  91.0 11.7 %cholesky.16 = f32[128,128]{1,0:T(8,128)S(1)} custom-call(f32[128,128]{1,0:T(8,128)S(1)} %fusion.1), custom_call_target="Cholesky" | custom-call | tf_op jit(solution)/shard_map/jit(cholesky)/cholesky | solution.py:119
  104.1 9.8 %custom-call.7 = f32[1,128,128]{1,2,0:T(8,128)S(1)} custom-call(f32[1,128,128]{2,1,0:T(8,128)S(1)} %get-tuple-element.13), custom_call_target="InvertDiagBlocksLowerTriangular" | custom-call | tf_op jit(solution)/shard_map/jit(_solve_triangular)/triangular_solve | solution.py:120
  (43 shorter events, 12.3 us)
Async XLA Ops:
  0.6 78.6 %copy-start.1 = (f32[512]{0:T(512)S(1)}, f32[512]{0:T(512)}, u32[]{:S(2)}) copy-start(f32[512]{0:T(512)} %param.8) | copy-start | bytes 6148
  1.7 15.9 %collective-permute-start = (bf16[512,128]{1,0:T(8,128)(2,1)S(1)}, bf16[512,128]{1,0:T(8,128)(2,1)S(1)}, u32[]{:S(2)}, u32[]{:S(2)}) collective-permute-start(bf16[512,128]{1,0:T(8,128)(2,1)S(1)} %multiply_convert_fusion), channel_id=1, source_target_pairs={{0,3},{1,4},{2,5},{3,6},{4,7},{8,11},{9,12},{10,13},{11,14},{12,15... | collective-permute-start | bytes 393224 | tf_op jit(solution)/shard_map/ppermute | solution.py:74
  6.1 12.8 %collective-permute-start.1 = (bf16[512,128]{1,0:T(8,128)(2,1)S(1)}, bf16[512,128]{1,0:T(8,128)(2,1)S(1)}, u32[]{:S(2)}, u32[]{:S(2)}) collective-permute-start(bf16[512,128]{1,0:T(8,128)(2,1)S(1)} %multiply_convert_fusion), channel_id=1, source_target_pairs={{0,2},{1,3},{2,4},{3,5},{4,6},{5,7},{8,10},{9,11},{10,12},{11,13},... | collective-permute-start | bytes 393224 | tf_op jit(solution)/shard_map/ppermute | solution.py:74
  9.6 9.4 %collective-permute-start.2 = (bf16[512,128]{1,0:T(8,128)(2,1)S(1)}, bf16[512,128]{1,0:T(8,128)(2,1)S(1)}, u32[]{:S(2)}, u32[]{:S(2)}) collective-permute-start(bf16[512,128]{1,0:T(8,128)(2,1)S(1)} %multiply_convert_fusion), channel_id=1, source_target_pairs={{0,1},{1,2},{2,3},{3,4},{4,5},{5,6},{6,7},{8,9},{9,10},{10,11},{11... | collective-permute-start | bytes 393224 | tf_op jit(solution)/shard_map/ppermute | solution.py:74
  12.9 7.1 %collective-permute-start.3 = (bf16[512,128]{1,0:T(8,128)(2,1)S(1)}, bf16[512,128]{1,0:T(8,128)(2,1)S(1)}, u32[]{:S(2)}, u32[]{:S(2)}) collective-permute-start(bf16[512,128]{1,0:T(8,128)(2,1)S(1)} %multiply_convert_fusion), channel_id=1, source_target_pairs={{1,0},{2,1},{3,2},{4,3},{5,4},{6,5},{7,6},{9,8},{10,9},{11,10},{12... | collective-permute-start | bytes 393224 | tf_op jit(solution)/shard_map/ppermute | solution.py:74
  14.2 8.4 %collective-permute-start.4 = (bf16[512,128]{1,0:T(8,128)(2,1)S(1)}, bf16[512,128]{1,0:T(8,128)(2,1)S(1)}, u32[]{:S(2)}, u32[]{:S(2)}) collective-permute-start(bf16[512,128]{1,0:T(8,128)(2,1)S(1)} %multiply_convert_fusion), channel_id=1, source_target_pairs={{2,0},{3,1},{4,2},{5,3},{6,4},{7,5},{10,8},{11,9},{12,10},{13,11},... | collective-permute-start | bytes 393224 | tf_op jit(solution)/shard_map/ppermute | solution.py:74
  17.6 7.6 %collective-permute-start.5 = (bf16[512,128]{1,0:T(8,128)(2,1)S(1)}, bf16[512,128]{1,0:T(8,128)(2,1)S(1)}, u32[]{:S(2)}, u32[]{:S(2)}) collective-permute-start(bf16[512,128]{1,0:T(8,128)(2,1)S(1)} %multiply_convert_fusion), channel_id=1, source_target_pairs={{3,0},{4,1},{5,2},{6,3},{7,4},{11,8},{12,9},{13,10},{14,11},{15,12... | collective-permute-start | bytes 393224 | tf_op jit(solution)/shard_map/ppermute | solution.py:74
  25.2 0.7 copy-start
  48.5 11.8 %collective-permute-start.10 = (bf16[4,128,128]{2,1,0:T(8,128)(2,1)S(1)}, bf16[4,128,128]{2,1,0:T(8,128)(2,1)S(1)}, u32[]{:S(2)}, u32[]{:S(2)}) collective-permute-start(bf16[4,128,128]{2,1,0:T(8,128)(2,1)S(1)} %get-tuple-element.8), channel_id=1, source_target_pairs={{0,2},{1,3},{2,4},{3,5},{4,6},{5,7},{8,10},{9,11},{10,12},{11,13},... | collective-permute-start | bytes 393224 | tf_op jit(solution)/shard_map/ppermute | solution.py:74
  54.0 9.6 %collective-permute-start.11 = (bf16[4,128,128]{2,1,0:T(8,128)(2,1)S(1)}, bf16[4,128,128]{2,1,0:T(8,128)(2,1)S(1)}, u32[]{:S(2)}, u32[]{:S(2)}) collective-permute-start(bf16[4,128,128]{2,1,0:T(8,128)(2,1)S(1)} %get-tuple-element.7), channel_id=1, source_target_pairs={{0,3},{1,4},{2,5},{3,6},{4,7},{8,11},{9,12},{10,13},{11,14},{12,15... | collective-permute-start | bytes 393224 | tf_op jit(solution)/shard_map/ppermute | solution.py:74
  56.4 7.2 %collective-permute-start.6 = (bf16[4,128,128]{2,1,0:T(8,128)(2,1)S(1)}, bf16[4,128,128]{2,1,0:T(8,128)(2,1)S(1)}, u32[]{:S(2)}, u32[]{:S(2)}) collective-permute-start(bf16[4,128,128]{2,1,0:T(8,128)(2,1)S(1)} %get-tuple-element.6), channel_id=1, source_target_pairs={{3,0},{4,1},{5,2},{6,3},{7,4},{11,8},{12,9},{13,10},{14,11},{15,12... | collective-permute-start | bytes 393224 | tf_op jit(solution)/shard_map/ppermute | solution.py:74
  57.7 9.6 %collective-permute-start.7 = (bf16[4,128,128]{2,1,0:T(8,128)(2,1)S(1)}, bf16[4,128,128]{2,1,0:T(8,128)(2,1)S(1)}, u32[]{:S(2)}, u32[]{:S(2)}) collective-permute-start(bf16[4,128,128]{2,1,0:T(8,128)(2,1)S(1)} %get-tuple-element.11), channel_id=1, source_target_pairs={{2,0},{3,1},{4,2},{5,3},{6,4},{7,5},{10,8},{11,9},{12,10},{13,11},... | collective-permute-start | bytes 393224 | tf_op jit(solution)/shard_map/ppermute | solution.py:74
  59.0 8.3 %collective-permute-start.8 = (bf16[4,128,128]{2,1,0:T(8,128)(2,1)S(1)}, bf16[4,128,128]{2,1,0:T(8,128)(2,1)S(1)}, u32[]{:S(2)}, u32[]{:S(2)}) collective-permute-start(bf16[4,128,128]{2,1,0:T(8,128)(2,1)S(1)} %get-tuple-element.10), channel_id=1, source_target_pairs={{1,0},{2,1},{3,2},{4,3},{5,4},{6,5},{7,6},{9,8},{10,9},{11,10},{12... | collective-permute-start | bytes 393224 | tf_op jit(solution)/shard_map/ppermute | solution.py:74
  60.3 7.0 %collective-permute-start.9 = (bf16[4,128,128]{2,1,0:T(8,128)(2,1)S(1)}, bf16[4,128,128]{2,1,0:T(8,128)(2,1)S(1)}, u32[]{:S(2)}, u32[]{:S(2)}) collective-permute-start(bf16[4,128,128]{2,1,0:T(8,128)(2,1)S(1)} %get-tuple-element.9), channel_id=1, source_target_pairs={{0,1},{1,2},{2,3},{3,4},{4,5},{5,6},{6,7},{8,9},{9,10},{10,11},{11... | collective-permute-start | bytes 393224 | tf_op jit(solution)/shard_map/ppermute | solution.py:74
  67.5 6.2 %collective-permute-start.12 = (bf16[4,128,128]{2,1,0:T(8,128)(2,1)S(1)}, bf16[4,128,128]{2,1,0:T(8,128)(2,1)S(1)}, u32[]{:S(2)}, u32[]{:S(2)}) collective-permute-start(bf16[4,128,128]{2,1,0:T(8,128)(2,1)S(1)} %add_convert_fusion.1), channel_id=1, source_target_pairs={{0,8},{8,0},{16,24},{24,16},{1,9},{9,1},{17,25},{25,17},{2,10},{10... | collective-permute-start | bytes 393224 | tf_op jit(solution)/shard_map/ppermute | solution.py:82
  73.7 5.6 %collective-permute-start.13 = (bf16[4,128,128]{2,1,0:T(8,128)(2,1)S(1)}, bf16[4,128,128]{2,1,0:T(8,128)(2,1)S(1)}, u32[]{:S(2)}, u32[]{:S(2)}) collective-permute-start(bf16[4,128,128]{2,1,0:T(8,128)(2,1)S(1)} %add_convert_fusion), channel_id=1, source_target_pairs={{0,16},{8,24},{16,0},{24,8},{1,17},{9,25},{17,1},{25,9},{2,18},{10... | collective-permute-start | bytes 393224 | tf_op jit(solution)/shard_map/ppermute | solution.py:82
  79.7 1.3 %collective-permute-start.14 = (f32[128,128]{0,1:T(8,128)S(1)}, f32[128,128]{0,1:T(8,128)S(1)}, u32[]{:S(2)}, u32[]{:S(2)}) collective-permute-start(f32[128,128]{0,1:T(8,128)S(1)} %convolution_bitcast_fusion), channel_id=1, source_target_pairs={{0,1},{1,0},{2,3},{3,2},{4,5},{5,4},{6,7},{7,6},{8,9},{9,8},{10,11... | collective-permute-start | bytes 196616 | tf_op jit(solution)/shard_map/ppermute | solution.py:82
  81.0 4.3 %collective-permute-start.15 = (f32[128,128]{0,1:T(8,128)S(1)}, f32[128,128]{0,1:T(8,128)S(1)}, u32[]{:S(2)}, u32[]{:S(2)}) collective-permute-start(f32[128,128]{0,1:T(8,128)S(1)} %add.54), channel_id=1, source_target_pairs={{0,2},{1,3},{2,0},{3,1},{4,6},{5,7},{6,4},{7,5},{8,10},{9,11},{10,... | collective-permute-start | bytes 196616 | tf_op jit(solution)/shard_map/ppermute | solution.py:82
  85.4 5.5 %collective-permute-start.16 = (f32[128,128]{0,1:T(8,128)S(1)}, f32[128,128]{0,1:T(8,128)S(1)}, u32[]{:S(2)}, u32[]{:S(2)}) collective-permute-start(f32[128,128]{0,1:T(8,128)S(1)} %add.55), channel_id=1, source_target_pairs={{0,4},{1,5},{2,6},{3,7},{4,0},{5,1},{6,2},{7,3},{8,12},{9,13},{10,... | collective-permute-start | bytes 196616 | tf_op jit(solution)/shard_map/ppermute | solution.py:82

commit v3 on v2

--- a/solution.py
+++ b/solution.py
@@ -68,6 +68,61 @@
         )(ray, cell, count, win, noise, tiles)
 
 
+def finish_kernel(root, gram_ref, sample_ref, basis_ref, factor_ref, work):
+    n = gram_ref.shape[0]
+    row_at = lax.broadcasted_iota(jnp.int32, (n, n), 0)
+    col_at = lax.broadcasted_iota(jnp.int32, (n, n), 1)
+    work[:, :n] = gram_ref[...]
+    work[:, n:] = jnp.where(row_at == col_at, 1.0, 0.0)
+    inside = lax.broadcasted_iota(jnp.int32, (8, n), 0)
+    for first in range(0, n, 8):
+        panel = work[first : first + 8, :]
+        cols = [
+            jnp.broadcast_to(panel[:, first + i : first + i + 1], (8, n)) for i in range(8)
+        ]
+        halves = [panel[:, :n], panel[:, n:]]
+        for i in range(8):
+            scale = lax.rsqrt(jnp.broadcast_to(cols[i][i : i + 1, :], (8, n)))
+            coef = jnp.where(inside > i, cols[i] * scale, 0.0)
+            for j in range(i + 1, 8):
+                cols[j] = cols[j] - coef * (cols[j][i : i + 1, :] * scale)
+            for h in range(2):
+                pivot = halves[h][i : i + 1, :] * scale
+                halves[h] = jnp.where(inside == i, pivot, halves[h] - coef * pivot)
+        panel = jnp.concatenate(halves, axis=1)
+        work[first : first + 8, :] = panel
+        if first + 8 < n:
+            update = lax.dot_general(
+                panel[:, :n],
+                panel,
+                (((0,), (0,)), ((), ())),
+                precision=lax.Precision.HIGHEST,
+                preferred_element_type=jnp.float32,
+            )
+            work[first + 8 :, :] = work[first + 8 :, :] - update[first + 8 :, :]
+    factor_ref[...] = jnp.where(row_at <= col_at, work[:, :n], 0.0) / root
+    inverse = jnp.where(row_at >= col_at, work[:, n:], 0.0)
+    rows = jnp.dot(
+        inverse, sample_ref[...], precision=lax.Precision.HIGHEST, preferred_element_type=jnp.float32
+    )
+    basis_ref[...] = rows.T * root
+
+
+def finish(gram, sample, root):
+    n, rows = sample.shape
+    return pl.pallas_call(
+        functools.partial(finish_kernel, root),
+        out_shape=(
+            jax.ShapeDtypeStruct((rows, n), jnp.float32),
+            jax.ShapeDtypeStruct((n, n), jnp.float32),
+        ),
+        in_specs=[pl.BlockSpec(memory_space=pltpu.VMEM)] * 2,
+        out_specs=(pl.BlockSpec(memory_space=pltpu.VMEM),) * 2,
+        scratch_shapes=[pltpu.VMEM((n, 2 * n), jnp.float32)],
+        compiler_params=pltpu.CompilerParams(vmem_limit_bytes=16 * 2**20),
+    )(gram, sample)
+
+
 def passed_along(value, axis, by):
     length = lax.axis_size(axis)
     pairs = [(i, i + by) for i in range(length) if 0 <= i + by < length]
@@ -111,14 +166,12 @@
     for d in range(-REACH, REACH + 1):
         if d != 0:
             own = own + passed_along(partial[REACH + d], "cell", d).astype(jnp.float32)
-    root_cells = jnp.sqrt(jnp.float32(own_rows * owner_total))
+    root_cells = float(own_rows * owner_total) ** 0.5
     gradient = summed(own, "ray", jnp.bfloat16)
     sample = prior.reshape(own_blocks, 1, edge) * gradient
     sample = sample.transpose(1, 0, 2).reshape(width, own_rows)
     gram = summed(jnp.dot(sample, sample.T, precision=lax.Precision.HIGHEST), "cell")
-    lower = jnp.linalg.cholesky(gram)
-    basis = jax.scipy.linalg.solve_triangular(lower, sample, lower=True).T
-    return (basis * root_cells, lower.T / root_cells)
+    return finish(gram, sample, root_cells)
 
 
 def solution(mesh):

time: 116 us -> 101 us (0.87)
  other arithmetic: 26.6 us -> 3.74 us
  Pallas kernels: 22.5 us -> 32.1 us
    another operation x4 -> x0, other arithmetic: 22.2 us -> none  [the longest x3 12.4 us: local(): lower = jnp.linalg.cholesky(gram)]
    pallas_call x0 -> x1, Pallas kernels: none -> 9.62 us  [finish(): pl.pallas_call(functools.partial(finish_kernel, root), out_shape=(jax.Sha...]
  transfers between devices with their start and end apart: 17 -> 17, of which waited for: 8 -> 8; matrix products, arithmetic and copies ran while one was open for 2% -> 3% of each run, Pallas kernels for 0% -> 0%
where the time goes in v3:
time: 101 us; the launch traced here: 100 us
  starting transfers between devices  37.8 us (37%)
  Pallas kernels  32.1 us (32%)
  waiting for transfers between devices  24 us (24%)
  other arithmetic  3.74 us (4%)
  between operations  1.57 us (2%)
    ppermute x12, starting transfers between devices, passed_along(): return lax.ppermute(value, axis, pairs)  30 us
    pallas_call x1, Pallas kernels, k2(): pl.pallas_call(functools.partial(k2_kernel, group, chunk), out_shape=jax....  22.5 us
    ppermute x5, waiting for transfers between devices, summed(): got = lax.ppermute(sent, axis, [(i, i ^ step) for i in range(length)])  15.1 us
    pallas_call x1, Pallas kernels, finish(): pl.pallas_call(functools.partial(finish_kernel, root), out_shape=(jax.Sha...  9.62 us
    ppermute x12, waiting for transfers between devices, passed_along(): return lax.ppermute(value, axis, pairs)  8.87 us
    ppermute x5, starting transfers between devices, summed(): got = lax.ppermute(sent, axis, [(i, i ^ step) for i in range(length)])  7.75 us
  transfers between devices with their start and end apart: 17, of which 8 were waited for; matrix products, arithmetic and copies ran while one was open for 3% of the time, Pallas kernels for 0%

profile of v3, /device:TPU:0, one launch (start us, length us, event | category | flops | bytes accessed | tf_op | source)
XLA Modules:
  0.0 100.5 jit_solution(8714418952975211845)
XLA Ops:
  1.7 4.4 %collective-permute-start = (bf16[512,128]{1,0:T(8,128)(2,1)S(1)}, bf16[512,128]{1,0:T(8,128)(2,1)S(1)}, u32[]{:S(2)}, u32[]{:S(2)}) collective-permute-start(bf16[512,128]{1,0:T(8,128)(2,1)S(1)} %multiply_convert_fusion), channel_id=1, source_target_pairs={{0,3},{1,4},{2,5},{3,6},{4,7},{8,11},{9,12},{10,13},{11,14},{12,15... | collective-permute-start | bytes 393224 | tf_op jit(solution)/shard_map/ppermute | solution.py:129
  6.1 3.5 %collective-permute-start.1 = (bf16[512,128]{1,0:T(8,128)(2,1)S(1)}, bf16[512,128]{1,0:T(8,128)(2,1)S(1)}, u32[]{:S(2)}, u32[]{:S(2)}) collective-permute-start(bf16[512,128]{1,0:T(8,128)(2,1)S(1)} %multiply_convert_fusion), channel_id=1, source_target_pairs={{0,2},{1,3},{2,4},{3,5},{4,6},{5,7},{8,10},{9,11},{10,12},{11,13},... | collective-permute-start | bytes 393224 | tf_op jit(solution)/shard_map/ppermute | solution.py:129
  9.6 3.3 %collective-permute-start.2 = (bf16[512,128]{1,0:T(8,128)(2,1)S(1)}, bf16[512,128]{1,0:T(8,128)(2,1)S(1)}, u32[]{:S(2)}, u32[]{:S(2)}) collective-permute-start(bf16[512,128]{1,0:T(8,128)(2,1)S(1)} %multiply_convert_fusion), channel_id=1, source_target_pairs={{0,1},{1,2},{2,3},{3,4},{4,5},{5,6},{6,7},{8,9},{9,10},{10,11},{11... | collective-permute-start | bytes 393224 | tf_op jit(solution)/shard_map/ppermute | solution.py:129
  12.9 1.3 %collective-permute-start.3 = (bf16[512,128]{1,0:T(8,128)(2,1)S(1)}, bf16[512,128]{1,0:T(8,128)(2,1)S(1)}, u32[]{:S(2)}, u32[]{:S(2)}) collective-permute-start(bf16[512,128]{1,0:T(8,128)(2,1)S(1)} %multiply_convert_fusion), channel_id=1, source_target_pairs={{1,0},{2,1},{3,2},{4,3},{5,4},{6,5},{7,6},{9,8},{10,9},{11,10},{12... | collective-permute-start | bytes 393224 | tf_op jit(solution)/shard_map/ppermute | solution.py:129
  14.2 1.3 %collective-permute-start.4 = (bf16[512,128]{1,0:T(8,128)(2,1)S(1)}, bf16[512,128]{1,0:T(8,128)(2,1)S(1)}, u32[]{:S(2)}, u32[]{:S(2)}) collective-permute-start(bf16[512,128]{1,0:T(8,128)(2,1)S(1)} %multiply_convert_fusion), channel_id=1, source_target_pairs={{2,0},{3,1},{4,2},{5,3},{6,4},{7,5},{10,8},{11,9},{12,10},{13,11},... | collective-permute-start | bytes 393224 | tf_op jit(solution)/shard_map/ppermute | solution.py:129
  20.1 2.5 %collective-permute-done.4 = bf16[512,128]{1,0:T(8,128)(2,1)S(1)} collective-permute-done((bf16[512,128]{1,0:T(8,128)(2,1)S(1)}, bf16[512,128]{1,0:T(8,128)(2,1)S(1)}, u32[]{:S(2)}, u32[]{:S(2)}) %collective-permute-start.4) | collective-permute-done | bytes 131104 | tf_op jit(solution)/shard_map/ppermute | solution.py:129
  22.6 2.6 %collective-permute-done.5 = bf16[512,128]{1,0:T(8,128)(2,1)S(1)} collective-permute-done((bf16[512,128]{1,0:T(8,128)(2,1)S(1)}, bf16[512,128]{1,0:T(8,128)(2,1)S(1)}, u32[]{:S(2)}, u32[]{:S(2)}) %collective-permute-start.5) | collective-permute-done | bytes 131104 | tf_op jit(solution)/shard_map/ppermute | solution.py:129
  25.9 22.5 %shard_map.86 = bf16[28,128,128]{2,1,0:T(8,128)(2,1)S(1)} custom-call(s32[720]{0:T(1024)S(1)} %reduce.ray_ref, s32[720]{0:T(1024)S(1)} %subtract_reduce_fusion.cell_ref, s32[1]{0:T(128)} %bitcast.15.count_ref, bf16[28,128,128]{2,1,0:T(8,128)(2,1)S(1)} %bitcast.16, f32[16,128]{1,0:T(8,128)S(1)} %bitcast.17, bf16[720,128,128]{2,1,0:T(8,128)(2,1)} %bitcast.18), custom_call_target="tpu_custom_call" | custom-call | tf_op jit(solution)/shard_map/pallas_call | solution.py:62
  48.5 5.5 %collective-permute-start.10 = (bf16[4,128,128]{2,1,0:T(8,128)(2,1)S(1)}, bf16[4,128,128]{2,1,0:T(8,128)(2,1)S(1)}, u32[]{:S(2)}, u32[]{:S(2)}) collective-permute-start(bf16[4,128,128]{2,1,0:T(8,128)(2,1)S(1)} %get-tuple-element.4), channel_id=1, source_target_pairs={{0,2},{1,3},{2,4},{3,5},{4,6},{5,7},{8,10},{9,11},{10,12},{11,13},... | collective-permute-start | bytes 393224 | tf_op jit(solution)/shard_map/ppermute | solution.py:129
  54.0 2.3 %collective-permute-start.11 = (bf16[4,128,128]{2,1,0:T(8,128)(2,1)S(1)}, bf16[4,128,128]{2,1,0:T(8,128)(2,1)S(1)}, u32[]{:S(2)}, u32[]{:S(2)}) collective-permute-start(bf16[4,128,128]{2,1,0:T(8,128)(2,1)S(1)} %get-tuple-element.3), channel_id=1, source_target_pairs={{0,3},{1,4},{2,5},{3,6},{4,7},{8,11},{9,12},{10,13},{11,14},{12,15... | collective-permute-start | bytes 393224 | tf_op jit(solution)/shard_map/ppermute | solution.py:129
  56.4 1.3 %collective-permute-start.6 = (bf16[4,128,128]{2,1,0:T(8,128)(2,1)S(1)}, bf16[4,128,128]{2,1,0:T(8,128)(2,1)S(1)}, u32[]{:S(2)}, u32[]{:S(2)}) collective-permute-start(bf16[4,128,128]{2,1,0:T(8,128)(2,1)S(1)} %get-tuple-element.2), channel_id=1, source_target_pairs={{3,0},{4,1},{5,2},{6,3},{7,4},{11,8},{12,9},{13,10},{14,11},{15,12... | collective-permute-start | bytes 393224 | tf_op jit(solution)/shard_map/ppermute | solution.py:129
  57.7 1.3 %collective-permute-start.7 = (bf16[4,128,128]{2,1,0:T(8,128)(2,1)S(1)}, bf16[4,128,128]{2,1,0:T(8,128)(2,1)S(1)}, u32[]{:S(2)}, u32[]{:S(2)}) collective-permute-start(bf16[4,128,128]{2,1,0:T(8,128)(2,1)S(1)} %get-tuple-element.7), channel_id=1, source_target_pairs={{2,0},{3,1},{4,2},{5,3},{6,4},{7,5},{10,8},{11,9},{12,10},{13,11},... | collective-permute-start | bytes 393224 | tf_op jit(solution)/shard_map/ppermute | solution.py:129
  59.0 1.3 %collective-permute-start.8 = (bf16[4,128,128]{2,1,0:T(8,128)(2,1)S(1)}, bf16[4,128,128]{2,1,0:T(8,128)(2,1)S(1)}, u32[]{:S(2)}, u32[]{:S(2)}) collective-permute-start(bf16[4,128,128]{2,1,0:T(8,128)(2,1)S(1)} %get-tuple-element.6), channel_id=1, source_target_pairs={{1,0},{2,1},{3,2},{4,3},{5,4},{6,5},{7,6},{9,8},{10,9},{11,10},{12... | collective-permute-start | bytes 393224 | tf_op jit(solution)/shard_map/ppermute | solution.py:129
  60.3 3.3 %collective-permute-start.9 = (bf16[4,128,128]{2,1,0:T(8,128)(2,1)S(1)}, bf16[4,128,128]{2,1,0:T(8,128)(2,1)S(1)}, u32[]{:S(2)}, u32[]{:S(2)}) collective-permute-start(bf16[4,128,128]{2,1,0:T(8,128)(2,1)S(1)} %get-tuple-element.5), channel_id=1, source_target_pairs={{0,1},{1,2},{2,3},{3,4},{4,5},{5,6},{6,7},{8,9},{9,10},{10,11},{11... | collective-permute-start | bytes 393224 | tf_op jit(solution)/shard_map/ppermute | solution.py:129
  63.6 3.7 %collective-permute-done.7 = bf16[4,128,128]{2,1,0:T(8,128)(2,1)S(1)} collective-permute-done((bf16[4,128,128]{2,1,0:T(8,128)(2,1)S(1)}, bf16[4,128,128]{2,1,0:T(8,128)(2,1)S(1)}, u32[]{:S(2)}, u32[]{:S(2)}) %collective-permute-start.7) | collective-permute-done | bytes 131104 | tf_op jit(solution)/shard_map/ppermute | solution.py:129
  67.5 1.6 %collective-permute-start.12 = (bf16[4,128,128]{2,1,0:T(8,128)(2,1)S(1)}, bf16[4,128,128]{2,1,0:T(8,128)(2,1)S(1)}, u32[]{:S(2)}, u32[]{:S(2)}) collective-permute-start(bf16[4,128,128]{2,1,0:T(8,128)(2,1)S(1)} %add_convert_fusion.1), channel_id=1, source_target_pairs={{0,8},{8,0},{16,24},{24,16},{1,9},{9,1},{17,25},{25,17},{2,10},{10... | collective-permute-start | bytes 393224 | tf_op jit(solution)/shard_map/ppermute | solution.py:137
  69.0 4.6 %collective-permute-done.12 = bf16[4,128,128]{2,1,0:T(8,128)(2,1)S(1)} collective-permute-done((bf16[4,128,128]{2,1,0:T(8,128)(2,1)S(1)}, bf16[4,128,128]{2,1,0:T(8,128)(2,1)S(1)}, u32[]{:S(2)}, u32[]{:S(2)}) %collective-permute-start.12) | collective-permute-done | bytes 131104 | tf_op jit(solution)/shard_map/ppermute | solution.py:137
  73.7 1.6 %collective-permute-start.13 = (bf16[4,128,128]{2,1,0:T(8,128)(2,1)S(1)}, bf16[4,128,128]{2,1,0:T(8,128)(2,1)S(1)}, u32[]{:S(2)}, u32[]{:S(2)}) collective-permute-start(bf16[4,128,128]{2,1,0:T(8,128)(2,1)S(1)} %add_convert_fusion), channel_id=1, source_target_pairs={{0,16},{8,24},{16,0},{24,8},{1,17},{9,25},{17,1},{25,9},{2,18},{10... | collective-permute-start | bytes 393224 | tf_op jit(solution)/shard_map/ppermute | solution.py:137
  75.2 4.0 %collective-permute-done.13 = bf16[4,128,128]{2,1,0:T(8,128)(2,1)S(1)} collective-permute-done((bf16[4,128,128]{2,1,0:T(8,128)(2,1)S(1)}, bf16[4,128,128]{2,1,0:T(8,128)(2,1)S(1)}, u32[]{:S(2)}, u32[]{:S(2)}) %collective-permute-start.13) | collective-permute-done | bytes 131104 | tf_op jit(solution)/shard_map/ppermute | solution.py:137
  81.0 1.6 %collective-permute-start.15 = (f32[128,128]{1,0:T(8,128)S(1)}, f32[128,128]{1,0:T(8,128)S(1)}, u32[]{:S(2)}, u32[]{:S(2)}) collective-permute-start(f32[128,128]{1,0:T(8,128)S(1)} %add.42), channel_id=1, source_target_pairs={{0,2},{1,3},{2,0},{3,1},{4,6},{5,7},{6,4},{7,5},{8,10},{9,11},{10,... | collective-permute-start | bytes 196616 | tf_op jit(solution)/shard_map/ppermute | solution.py:137
  82.6 2.8 %collective-permute-done.15 = f32[128,128]{1,0:T(8,128)S(1)} collective-permute-done((f32[128,128]{1,0:T(8,128)S(1)}, f32[128,128]{1,0:T(8,128)S(1)}, u32[]{:S(2)}, u32[]{:S(2)}) %collective-permute-start.15) | collective-permute-done | bytes 65568 | tf_op jit(solution)/shard_map/ppermute | solution.py:137
  85.3 2.9 %collective-permute-start.16 = (f32[128,128]{1,0:T(8,128)S(1)}, f32[128,128]{1,0:T(8,128)S(1)}, u32[]{:S(2)}, u32[]{:S(2)}) collective-permute-start(f32[128,128]{1,0:T(8,128)S(1)} %add.43), channel_id=1, source_target_pairs={{0,4},{1,5},{2,6},{3,7},{4,0},{5,1},{6,2},{7,3},{8,12},{9,13},{10,... | collective-permute-start | bytes 196616 | tf_op jit(solution)/shard_map/ppermute | solution.py:137
  88.3 2.5 %collective-permute-done.16 = f32[128,128]{1,0:T(8,128)S(1)} collective-permute-done((f32[128,128]{1,0:T(8,128)S(1)}, f32[128,128]{1,0:T(8,128)S(1)}, u32[]{:S(2)}, u32[]{:S(2)}) %collective-permute-start.16) | collective-permute-done | bytes 65568 | tf_op jit(solution)/shard_map/ppermute | solution.py:137
  90.8 9.6 %shard_map.87 = (f32[512,128]{1,0:T(8,128)}, f32[128,128]{1,0:T(8,128)}) custom-call(f32[128,128]{1,0:T(8,128)S(1)} %add.44.gram_ref, f32[128,512]{1,0:T(8,128)S(1)} %copy_bitcast_fusion.sample_ref), custom_call_target="tpu_custom_call" | custom-call | tf_op jit(solution)/shard_map/pallas_call | solution.py:113
  (34 shorter events, 7.6 us)
Async XLA Ops:
  0.6 78.6 %copy-start.1 = (f32[512]{0:T(512)S(1)}, f32[512]{0:T(512)}, u32[]{:S(2)}) copy-start(f32[512]{0:T(512)} %param.8) | copy-start | bytes 6148
  1.7 15.9 %collective-permute-start = (bf16[512,128]{1,0:T(8,128)(2,1)S(1)}, bf16[512,128]{1,0:T(8,128)(2,1)S(1)}, u32[]{:S(2)}, u32[]{:S(2)}) collective-permute-start(bf16[512,128]{1,0:T(8,128)(2,1)S(1)} %multiply_convert_fusion), channel_id=1, source_target_pairs={{0,3},{1,4},{2,5},{3,6},{4,7},{8,11},{9,12},{10,13},{11,14},{12,15... | collective-permute-start | bytes 393224 | tf_op jit(solution)/shard_map/ppermute | solution.py:129
  6.1 12.8 %collective-permute-start.1 = (bf16[512,128]{1,0:T(8,128)(2,1)S(1)}, bf16[512,128]{1,0:T(8,128)(2,1)S(1)}, u32[]{:S(2)}, u32[]{:S(2)}) collective-permute-start(bf16[512,128]{1,0:T(8,128)(2,1)S(1)} %multiply_convert_fusion), channel_id=1, source_target_pairs={{0,2},{1,3},{2,4},{3,5},{4,6},{5,7},{8,10},{9,11},{10,12},{11,13},... | collective-permute-start | bytes 393224 | tf_op jit(solution)/shard_map/ppermute | solution.py:129
  9.6 9.4 %collective-permute-start.2 = (bf16[512,128]{1,0:T(8,128)(2,1)S(1)}, bf16[512,128]{1,0:T(8,128)(2,1)S(1)}, u32[]{:S(2)}, u32[]{:S(2)}) collective-permute-start(bf16[512,128]{1,0:T(8,128)(2,1)S(1)} %multiply_convert_fusion), channel_id=1, source_target_pairs={{0,1},{1,2},{2,3},{3,4},{4,5},{5,6},{6,7},{8,9},{9,10},{10,11},{11... | collective-permute-start | bytes 393224 | tf_op jit(solution)/shard_map/ppermute | solution.py:129
  12.9 7.1 %collective-permute-start.3 = (bf16[512,128]{1,0:T(8,128)(2,1)S(1)}, bf16[512,128]{1,0:T(8,128)(2,1)S(1)}, u32[]{:S(2)}, u32[]{:S(2)}) collective-permute-start(bf16[512,128]{1,0:T(8,128)(2,1)S(1)} %multiply_convert_fusion), channel_id=1, source_target_pairs={{1,0},{2,1},{3,2},{4,3},{5,4},{6,5},{7,6},{9,8},{10,9},{11,10},{12... | collective-permute-start | bytes 393224 | tf_op jit(solution)/shard_map/ppermute | solution.py:129
  14.2 8.4 %collective-permute-start.4 = (bf16[512,128]{1,0:T(8,128)(2,1)S(1)}, bf16[512,128]{1,0:T(8,128)(2,1)S(1)}, u32[]{:S(2)}, u32[]{:S(2)}) collective-permute-start(bf16[512,128]{1,0:T(8,128)(2,1)S(1)} %multiply_convert_fusion), channel_id=1, source_target_pairs={{2,0},{3,1},{4,2},{5,3},{6,4},{7,5},{10,8},{11,9},{12,10},{13,11},... | collective-permute-start | bytes 393224 | tf_op jit(solution)/shard_map/ppermute | solution.py:129
  17.6 7.6 %collective-permute-start.5 = (bf16[512,128]{1,0:T(8,128)(2,1)S(1)}, bf16[512,128]{1,0:T(8,128)(2,1)S(1)}, u32[]{:S(2)}, u32[]{:S(2)}) collective-permute-start(bf16[512,128]{1,0:T(8,128)(2,1)S(1)} %multiply_convert_fusion), channel_id=1, source_target_pairs={{3,0},{4,1},{5,2},{6,3},{7,4},{11,8},{12,9},{13,10},{14,11},{15,12... | collective-permute-start | bytes 393224 | tf_op jit(solution)/shard_map/ppermute | solution.py:129
  25.2 0.7 copy-start
  48.5 11.8 %collective-permute-start.10 = (bf16[4,128,128]{2,1,0:T(8,128)(2,1)S(1)}, bf16[4,128,128]{2,1,0:T(8,128)(2,1)S(1)}, u32[]{:S(2)}, u32[]{:S(2)}) collective-permute-start(bf16[4,128,128]{2,1,0:T(8,128)(2,1)S(1)} %get-tuple-element.4), channel_id=1, source_target_pairs={{0,2},{1,3},{2,4},{3,5},{4,6},{5,7},{8,10},{9,11},{10,12},{11,13},... | collective-permute-start | bytes 393224 | tf_op jit(solution)/shard_map/ppermute | solution.py:129
  54.0 9.5 %collective-permute-start.11 = (bf16[4,128,128]{2,1,0:T(8,128)(2,1)S(1)}, bf16[4,128,128]{2,1,0:T(8,128)(2,1)S(1)}, u32[]{:S(2)}, u32[]{:S(2)}) collective-permute-start(bf16[4,128,128]{2,1,0:T(8,128)(2,1)S(1)} %get-tuple-element.3), channel_id=1, source_target_pairs={{0,3},{1,4},{2,5},{3,6},{4,7},{8,11},{9,12},{10,13},{11,14},{12,15... | collective-permute-start | bytes 393224 | tf_op jit(solution)/shard_map/ppermute | solution.py:129
  56.4 7.2 %collective-permute-start.6 = (bf16[4,128,128]{2,1,0:T(8,128)(2,1)S(1)}, bf16[4,128,128]{2,1,0:T(8,128)(2,1)S(1)}, u32[]{:S(2)}, u32[]{:S(2)}) collective-permute-start(bf16[4,128,128]{2,1,0:T(8,128)(2,1)S(1)} %get-tuple-element.2), channel_id=1, source_target_pairs={{3,0},{4,1},{5,2},{6,3},{7,4},{11,8},{12,9},{13,10},{14,11},{15,12... | collective-permute-start | bytes 393224 | tf_op jit(solution)/shard_map/ppermute | solution.py:129
  57.7 9.6 %collective-permute-start.7 = (bf16[4,128,128]{2,1,0:T(8,128)(2,1)S(1)}, bf16[4,128,128]{2,1,0:T(8,128)(2,1)S(1)}, u32[]{:S(2)}, u32[]{:S(2)}) collective-permute-start(bf16[4,128,128]{2,1,0:T(8,128)(2,1)S(1)} %get-tuple-element.7), channel_id=1, source_target_pairs={{2,0},{3,1},{4,2},{5,3},{6,4},{7,5},{10,8},{11,9},{12,10},{13,11},... | collective-permute-start | bytes 393224 | tf_op jit(solution)/shard_map/ppermute | solution.py:129
  59.0 8.3 %collective-permute-start.8 = (bf16[4,128,128]{2,1,0:T(8,128)(2,1)S(1)}, bf16[4,128,128]{2,1,0:T(8,128)(2,1)S(1)}, u32[]{:S(2)}, u32[]{:S(2)}) collective-permute-start(bf16[4,128,128]{2,1,0:T(8,128)(2,1)S(1)} %get-tuple-element.6), channel_id=1, source_target_pairs={{1,0},{2,1},{3,2},{4,3},{5,4},{6,5},{7,6},{9,8},{10,9},{11,10},{12... | collective-permute-start | bytes 393224 | tf_op jit(solution)/shard_map/ppermute | solution.py:129
  60.3 7.0 %collective-permute-start.9 = (bf16[4,128,128]{2,1,0:T(8,128)(2,1)S(1)}, bf16[4,128,128]{2,1,0:T(8,128)(2,1)S(1)}, u32[]{:S(2)}, u32[]{:S(2)}) collective-permute-start(bf16[4,128,128]{2,1,0:T(8,128)(2,1)S(1)} %get-tuple-element.5), channel_id=1, source_target_pairs={{0,1},{1,2},{2,3},{3,4},{4,5},{5,6},{6,7},{8,9},{9,10},{10,11},{11... | collective-permute-start | bytes 393224 | tf_op jit(solution)/shard_map/ppermute | solution.py:129
  67.5 6.2 %collective-permute-start.12 = (bf16[4,128,128]{2,1,0:T(8,128)(2,1)S(1)}, bf16[4,128,128]{2,1,0:T(8,128)(2,1)S(1)}, u32[]{:S(2)}, u32[]{:S(2)}) collective-permute-start(bf16[4,128,128]{2,1,0:T(8,128)(2,1)S(1)} %add_convert_fusion.1), channel_id=1, source_target_pairs={{0,8},{8,0},{16,24},{24,16},{1,9},{9,1},{17,25},{25,17},{2,10},{10... | collective-permute-start | bytes 393224 | tf_op jit(solution)/shard_map/ppermute | solution.py:137
  73.7 5.6 %collective-permute-start.13 = (bf16[4,128,128]{2,1,0:T(8,128)(2,1)S(1)}, bf16[4,128,128]{2,1,0:T(8,128)(2,1)S(1)}, u32[]{:S(2)}, u32[]{:S(2)}) collective-permute-start(bf16[4,128,128]{2,1,0:T(8,128)(2,1)S(1)} %add_convert_fusion), channel_id=1, source_target_pairs={{0,16},{8,24},{16,0},{24,8},{1,17},{9,25},{17,1},{25,9},{2,18},{10... | collective-permute-start | bytes 393224 | tf_op jit(solution)/shard_map/ppermute | solution.py:137
  79.7 1.3 %collective-permute-start.14 = (f32[128,128]{1,0:T(8,128)S(1)}, f32[128,128]{1,0:T(8,128)S(1)}, u32[]{:S(2)}, u32[]{:S(2)}) collective-permute-start(f32[128,128]{1,0:T(8,128)S(1)} %convolution_bitcast_fusion), channel_id=1, source_target_pairs={{0,1},{1,0},{2,3},{3,2},{4,5},{5,4},{6,7},{7,6},{8,9},{9,8},{10,11... | collective-permute-start | bytes 196616 | tf_op jit(solution)/shard_map/ppermute | solution.py:137
  81.0 4.3 %collective-permute-start.15 = (f32[128,128]{1,0:T(8,128)S(1)}, f32[128,128]{1,0:T(8,128)S(1)}, u32[]{:S(2)}, u32[]{:S(2)}) collective-permute-start(f32[128,128]{1,0:T(8,128)S(1)} %add.42), channel_id=1, source_target_pairs={{0,2},{1,3},{2,0},{3,1},{4,6},{5,7},{6,4},{7,5},{8,10},{9,11},{10,... | collective-permute-start | bytes 196616 | tf_op jit(solution)/shard_map/ppermute | solution.py:137
  85.3 5.5 %collective-permute-start.16 = (f32[128,128]{1,0:T(8,128)S(1)}, f32[128,128]{1,0:T(8,128)S(1)}, u32[]{:S(2)}, u32[]{:S(2)}) collective-permute-start(f32[128,128]{1,0:T(8,128)S(1)} %add.43), channel_id=1, source_target_pairs={{0,4},{1,5},{2,6},{3,7},{4,0},{5,1},{6,2},{7,3},{8,12},{9,13},{10,... | collective-permute-start | bytes 196616 | tf_op jit(solution)/shard_map/ppermute | solution.py:137
